TPU v7x, 32 devices: a whole 2x2x4 slice. The times are simulated.
32 devices in a mesh: dp: 4 (over x, core), adapter: 8 (over z, y).
Axes of the slice: x: 2, y: 2, z: 4, core: 2. Of those that a mesh axis runs over, the one named last changes fastest.
Arguments:
- tokens: bfloat16 [4096, 8192], P(('dp', 'adapter')), may hold values from -6 to 6
- token_adapter_index: int32 [4096, 1], P(('dp', 'adapter')), may hold values from 0 to 31; in each aligned block of 128 rows (0 to 127, 128 to 255, ...) at most 8 rows name the same one
- frozen_value_weight: bfloat16 [8192, 1024], P('dp'), may hold values from -0.0625 to 0.0625
- adapter_down_factors: bfloat16 [128, 16, 8192], P(('dp', 'adapter')), may hold values from -0.0625 to 0.0625
- adapter_up_factors: bfloat16 [128, 16, 1024], P(('dp', 'adapter')), may hold values from -1.5 to 1.5
- output_gradient: bfloat16 [4096, 1024], P(('dp', 'adapter')), may hold values from -6 to 6
Outputs:
- result: bfloat16 [4096, 1024], P(('dp', 'adapter'))
- token_grad: bfloat16 [4096, 8192], P(('dp', 'adapter'))
- down_grad: float32 [128, 16, 8192], P(('dp', 'adapter'))
- up_factor_gradient: float32 [128, 16, 1024], P(('dp', 'adapter'))
Inputs may be any that keep to these rules, and one draw needn't show every extreme that they name: `token_adapter_index`: among one device's 128 tokens no adapter id appears more than 8 times; in some device one appears exactly 8 times.
All inputs are finite; a program needn't handle non-finite values.
Results may differ from a plain program's by a relative error of at most 0.0054.
Values may be sent and summed in bfloat16 or wider, within the bound.
A program may use at most 128 MiB of HBM per device.

v0:
```python
import jax
import jax.numpy as jnp
from jax import lax
from jax.sharding import PartitionSpec as P

adapter_scale = 2.0


def placing_matrix(token_adapter_index, group_count, most):
    adapter_index = token_adapter_index[:, 0]
    onehot = (adapter_index[:, None] == jnp.arange(group_count, dtype=jnp.int32)[None, :]).astype(
        jnp.int32
    )
    ranks = jnp.sum(onehot * (jnp.cumsum(onehot, axis=0) - 1), axis=1)
    slot_of = adapter_index * most + ranks
    slot_total = group_count * most
    return (jnp.arange(slot_total, dtype=jnp.int32)[:, None] == slot_of[None, :]).astype(
        jnp.bfloat16
    )


def spread_rows(placing, rows, owners):
    packed = jnp.dot(placing, rows, preferred_element_type=jnp.float32).astype(jnp.bfloat16)
    return packed.reshape(owners, -1, rows.shape[1])


def collect_rows(placing, packed):
    flat = packed.reshape(-1, packed.shape[-1])
    return jnp.dot(placing.T, flat, preferred_element_type=jnp.float32)


def local(
    tokens,
    token_adapter_index,
    frozen_value_weight,
    adapter_down_factors,
    adapter_up_factors,
    output_gradient,
):
    owners = lax.axis_size("adapter")
    group_adapter_count = adapter_down_factors.shape[0]
    group_count = group_adapter_count * owners
    tok_rows = tokens.shape[0]
    most = max(2, 2 * tok_rows // group_count)
    width = tokens.shape[1]
    kv_width = output_gradient.shape[1]
    placing = placing_matrix(token_adapter_index, group_count, most)
    send_rows = spread_rows(placing, tokens, owners)
    send_grads = spread_rows(placing, output_gradient, owners)
    got_rows = lax.all_to_all(send_rows, "adapter", split_axis=0, concat_axis=0, tiled=True)
    reshaped_rows = got_rows.reshape(owners, group_adapter_count, most, width)
    rank_rows = jnp.einsum(
        "ofep,fqp->ofeq", reshaped_rows, adapter_down_factors, preferred_element_type=jnp.float32
    ).astype(jnp.bfloat16)
    raised_rows = (
        adapter_scale
        * jnp.einsum(
            "qaec,acn->qaen", rank_rows, adapter_up_factors, preferred_element_type=jnp.float32
        )
    ).astype(jnp.bfloat16)
    reshaped_rows, rank_rows, raised_rows = (
        reshaped_rows,
        rank_rows,
        raised_rows.reshape(owners, group_adapter_count * most, kv_width),
    )
    lifted_back = lax.all_to_all(raised_rows, "adapter", split_axis=0, concat_axis=0, tiled=True)
    got_grads = lax.all_to_all(send_grads, "adapter", split_axis=0, concat_axis=0, tiled=True)
    gradient_list = got_grads.reshape(owners, group_adapter_count, most, kv_width)
    rank_gradient = (
        adapter_scale
        * jnp.einsum(
            "thdu,hgu->thdg", gradient_list, adapter_up_factors, preferred_element_type=jnp.float32
        )
    ).astype(jnp.bfloat16)
    up_factor_gradient = adapter_scale * jnp.einsum(
        "sjmr,sjmk->jrk", rank_rows, gradient_list, preferred_element_type=jnp.float32
    )
    down_grad = jnp.einsum(
        "sjmr,sjmd->jrd", rank_gradient, reshaped_rows, preferred_element_type=jnp.float32
    )
    side = jnp.einsum(
        "elui,lip->elup", rank_gradient, adapter_down_factors, preferred_element_type=jnp.float32
    ).astype(jnp.bfloat16)
    down_grad, up_factor_gradient, side = (
        down_grad,
        up_factor_gradient,
        side.reshape(owners, group_adapter_count * most, width),
    )
    side_back = lax.all_to_all(side, "adapter", split_axis=0, concat_axis=0, tiled=True)
    lifted_tok = collect_rows(placing, lifted_back)
    side_tok = collect_rows(placing, side_back)
    whole_weight = lax.all_gather(frozen_value_weight, "dp", axis=0, tiled=True)
    base_out = jnp.dot(tokens, whole_weight, preferred_element_type=jnp.float32)
    base_back = lax.dot_general(
        output_gradient, whole_weight, (((1,), (1,)), ((), ())), preferred_element_type=jnp.float32
    )
    result = (base_out + lifted_tok).astype(jnp.bfloat16)
    token_grad = (base_back + side_tok).astype(jnp.bfloat16)
    return (result, token_grad, down_grad, up_factor_gradient)


def solution(mesh):
    in_specs = (
        P(("dp", "adapter"), None),
        P(("dp", "adapter"), None),
        P("dp", None),
        P(("dp", "adapter"), None, None),
        P(("dp", "adapter"), None, None),
        P(("dp", "adapter"), None),
    )
    out_specs = (
        P(("dp", "adapter"), None),
        P(("dp", "adapter"), None),
        P(("dp", "adapter"), None, None),
        P(("dp", "adapter"), None, None),
    )
    return jax.shard_map(local, mesh=mesh, in_specs=in_specs, out_specs=out_specs, check_vma=False)
```

profile of v0, /device:TPU:14, one launch (start us, length us, event | category | flops | bytes accessed | tf_op | source)
XLA Modules:
  0.0 250.5 jit_solution(9065447364600938227)
XLA Ops:
  7.2 0.0 copy-start
  7.2 0.0 copy-start.6
  7.2 0.0 copy-start.4
  7.2 0.0 all-gather.2.cloned.1.call-start
  7.2 0.7 all-gather.2.cloned.1.call-update
  7.9 0.1 copy-done.6
  8.0 0.1 fusion.27
  8.1 0.2 reduce_window_sum.11
  8.2 0.2 select_reduce_fusion
  8.4 0.0 copy-done.4
  8.4 1.1 convolution_convert_fusion.2
  9.5 6.2 %all-to-all-start.2 = ((bf16[8,32,1024]{2,1,0:T(8,128)(2,1)}), bf16[8,32,1024]{2,1,0:T(8,128)(2,1)S(1)}, u32[]{:S(2)}, u32[]{:S(2)}) async-start(bf16[8,32,1024]{2,1,0:T(8,128)(2,1)} %bitcast.11), calls=%async_computation.2 | async-start | bytes 1048576 | tf_op jit(solution)/shard_map/all_to_all | solution.py:67
  15.8 0.0 copy-done
  15.8 3.4 %convolution_convert_fusion.1 = bf16[256,8192]{1,0:T(8,128)(2,1)} fusion(bf16[128,8192]{1,0:T(8,128)(2,1)S(1)} %copy-done, s32[128]{0:T(128)S(1)} %multiply_add_fusion), kind=kOutput, calls=%fused_computation.1 | convolution fusion | flops 539000832 | bytes 6291968 | tf_op jit(solution)/shard_map/dot_general | solution.py:23
  19.1 7.9 %all-to-all-done.2 = bf16[8,32,1024]{2,1,0:T(8,128)(2,1)S(1)} async-done(((bf16[8,32,1024]{2,1,0:T(8,128)(2,1)}), bf16[8,32,1024]{2,1,0:T(8,128)(2,1)S(1)}, u32[]{:S(2)}, u32[]{:S(2)}) %all-to-all-start.2) | async-done | bytes 524320 | tf_op jit(solution)/shard_map/all_to_all | solution.py:67
  27.0 0.0 copy-start.2
  27.0 0.8 copy-done.2
  27.8 0.0 copy-start.1
  27.8 7.8 %all-to-all-start = ((bf16[8,32,8192]{2,1,0:T(8,128)(2,1)}), bf16[8,32,8192]{2,1,0:T(8,128)(2,1)}, u32[]{:S(2)}, u32[]{:S(2)}) async-start(bf16[8,32,8192]{2,1,0:T(8,128)(2,1)} %bitcast.69), calls=%async_computation | async-start | bytes 8388608 | tf_op jit(solution)/shard_map/all_to_all | solution.py:50
  35.6 1.4 fusion.16
  37.0 0.0 copy-done.1
  37.0 1.2 fusion
  38.3 2.2 copy.46
  40.5 84.4 %all-to-all-done = bf16[8,32,8192]{2,1,0:T(8,128)(2,1)} async-done(((bf16[8,32,8192]{2,1,0:T(8,128)(2,1)}), bf16[8,32,8192]{2,1,0:T(8,128)(2,1)}, u32[]{:S(2)}, u32[]{:S(2)}) %all-to-all-start) | async-done | bytes 4194336 | tf_op jit(solution)/shard_map/all_to_all | solution.py:50
  124.9 7.9 %all-to-all-start.3 = ((bf16[8,32,8192]{2,1,0:T(8,128)(2,1)}), bf16[8,32,8192]{2,1,0:T(8,128)(2,1)}, u32[]{:S(2)}, u32[]{:S(2)}) async-start(bf16[8,32,8192]{2,1,0:T(8,128)(2,1)} %bitcast.68), calls=%async_computation.3 | async-start | bytes 8388608 | tf_op jit(solution)/shard_map/all_to_all | solution.py:89
  132.7 0.0 copy-start.5
  132.8 0.0 copy-start.3
  132.8 3.5 %fusion.13 = bf16[8,4,8,16]{3,2,0,1:T(8,128)(2,1)S(1)} fusion(bf16[4,16,8192]{2,1,0:T(8,128)(2,1)S(1)} %copy-done.1, bf16[8,32,8192]{2,1,0:T(8,128)(2,1)} %all-to-all-done), kind=kOutput, calls=%fused_computation.21 | convolution fusion | flops 67112960 | bytes 5251072 | tf_op jit(solution)/shard_map/ofep,fqp->ofeq/dot_general | solution.py:52
  136.2 0.0 copy-done.5
  136.2 0.3 fusion.6
  136.5 0.9 copy.47
  137.4 0.0 copy-done.3
  137.4 1.0 fusion.8
  138.3 4.2 %convolution_bitcast_fusion = f32[4,16,8192]{2,1,0:T(8,128)} fusion(bf16[8,4,8,16]{3,2,0,1:T(8,128)(2,1)S(1)} %fusion.16, bf16[8,32,8192]{2,1,0:T(8,128)(2,1)} %all-to-all-done), kind=kOutput, calls=%fused_computation.5 | convolution fusion | flops 67108864 | bytes 6299648 | tf_op jit(solution)/shard_map/sjmr,sjmd->jrd/dot_general | solution.py:78
  142.6 0.0 all-gather.2.cloned.1.call-done
  142.6 13.3 %fusion.29 = f32[128,8192]{1,0:T(8,128)} fusion(bf16[128,1024]{1,0:T(8,128)(2,1)S(1)} %copy-done.4, bf16[8192,1024]{1,0:T(8,128)(2,1)} %all-gather.2.cloned.1.call-done), kind=kOutput, calls=%fused_computation.40 | convolution fusion | flops 2147483648 | bytes 21233664 | tf_op jit(solution)/shard_map/dot_general | solution.py:94
  155.9 66.1 %all-to-all-done.3 = bf16[8,32,8192]{2,1,0:T(8,128)(2,1)} async-done(((bf16[8,32,8192]{2,1,0:T(8,128)(2,1)}), bf16[8,32,8192]{2,1,0:T(8,128)(2,1)}, u32[]{:S(2)}, u32[]{:S(2)}) %all-to-all-start.3) | async-done | bytes 4194336 | tf_op jit(solution)/shard_map/all_to_all | solution.py:89
  222.0 7.0 %all-to-all-start.1 = ((bf16[8,32,1024]{2,1,0:T(8,128)(2,1)}), bf16[8,32,1024]{2,1,0:T(8,128)(2,1)S(1)}, u32[]{:S(2)}, u32[]{:S(2)}) async-start(bf16[8,32,1024]{2,1,0:T(8,128)(2,1)} %bitcast.67), calls=%async_computation.1 | async-start | bytes 1048576 | tf_op jit(solution)/shard_map/all_to_all | solution.py:66
  229.0 5.6 %fusion.1 = bf16[128,8192]{1,0:T(8,128)(2,1)} fusion(f32[128,8192]{1,0:T(8,128)} %fusion.29, bf16[256,8192]{1,0:T(8,128)(2,1)} %bitcast.18, s32[128]{0:T(128)S(1)} %multiply_add_fusion), kind=kOutput, calls=%fused_computation.4 | convolution fusion | flops 539000832 | bytes 10486272 | tf_op jit(solution)/shard_map/dot_general | solution.py:29
  234.6 8.1 %fusion.28 = f32[128,1024]{1,0:T(8,128)S(1)} fusion(bf16[128,8192]{1,0:T(8,128)(2,1)S(1)} %copy-done, bf16[8192,1024]{1,0:T(8,128)(2,1)} %all-gather.2.cloned.1.call-done), kind=kOutput, calls=%fused_computation.39 | convolution fusion | flops 2147483648 | bytes 19398656 | tf_op jit(solution)/shard_map/dot_general | solution.py:93
  242.7 0.0 all-to-all-done.1
  242.7 1.0 fusion.7
  (1 shorter events, 0.0 us)
Async XLA Ops:
  7.2 8.6 %copy-start = (bf16[128,8192]{1,0:T(8,128)(2,1)S(1)}, bf16[128,8192]{1,0:T(8,128)(2,1)}, u32[]{:S(2)}) copy-start(bf16[128,8192]{1,0:T(8,128)(2,1)} %param.6) | copy-start | bytes 6291460
  7.2 0.8 copy-start.6
  7.2 1.2 copy-start.4
  7.2 135.4 %all-gather.2.cloned.1.call-start = ((), (), s32[]{:S(2)}) async-start(), calls=%async_computation.4 | async-start | bytes 20971520 | tf_op jit(solution)/shard_map/all_gather | solution.py:92
  9.5 17.5 %all-to-all-start.2 = ((bf16[8,32,1024]{2,1,0:T(8,128)(2,1)}), bf16[8,32,1024]{2,1,0:T(8,128)(2,1)S(1)}, u32[]{:S(2)}, u32[]{:S(2)}) async-start(bf16[8,32,1024]{2,1,0:T(8,128)(2,1)} %bitcast.11), calls=%async_computation.2 | async-start | bytes 1048576 | tf_op jit(solution)/shard_map/all_to_all | solution.py:67
  27.0 0.8 copy-start.2
  27.8 9.2 %copy-start.1 = (bf16[4,16,8192]{2,1,0:T(8,128)(2,1)S(1)}, bf16[4,16,8192]{2,1,0:T(8,128)(2,1)}, u32[]{:S(2)}) copy-start(bf16[4,16,8192]{2,1,0:T(8,128)(2,1)} %param.9) | copy-start | bytes 3145732
  27.8 97.1 %all-to-all-start = ((bf16[8,32,8192]{2,1,0:T(8,128)(2,1)}), bf16[8,32,8192]{2,1,0:T(8,128)(2,1)}, u32[]{:S(2)}, u32[]{:S(2)}) async-start(bf16[8,32,8192]{2,1,0:T(8,128)(2,1)} %bitcast.69), calls=%async_computation | async-start | bytes 8388608 | tf_op jit(solution)/shard_map/all_to_all | solution.py:50
  124.9 97.1 %all-to-all-start.3 = ((bf16[8,32,8192]{2,1,0:T(8,128)(2,1)}), bf16[8,32,8192]{2,1,0:T(8,128)(2,1)}, u32[]{:S(2)}, u32[]{:S(2)}) async-start(bf16[8,32,8192]{2,1,0:T(8,128)(2,1)} %bitcast.68), calls=%async_computation.3 | async-start | bytes 8388608 | tf_op jit(solution)/shard_map/all_to_all | solution.py:89
  132.7 3.5 %copy-start.5 = (bf16[4,16,1024]{2,1,0:T(8,128)(2,1)S(1)}, bf16[4,16,1024]{2,1,0:T(8,128)(2,1)}, u32[]{:S(2)}) copy-start(bf16[4,16,1024]{2,1,0:T(8,128)(2,1)} %param.10) | copy-start | bytes 393220
  132.8 4.6 %copy-start.3 = (bf16[8,32,1024]{2,1,0:T(8,128)(2,1)S(1)}, bf16[8,32,1024]{2,1,0:T(8,128)(2,1)}, u32[]{:S(2)}) copy-start(bf16[8,32,1024]{2,1,0:T(8,128)(2,1)} %copy-done.2) | copy-start | bytes 1572868
  222.0 20.7 %all-to-all-start.1 = ((bf16[8,32,1024]{2,1,0:T(8,128)(2,1)}), bf16[8,32,1024]{2,1,0:T(8,128)(2,1)S(1)}, u32[]{:S(2)}, u32[]{:S(2)}) async-start(bf16[8,32,1024]{2,1,0:T(8,128)(2,1)} %bitcast.67), calls=%async_computation.1 | async-start | bytes 1048576 | tf_op jit(solution)/shard_map/all_to_all | solution.py:66
Sparse Core Ops, SparseCore 0:
  9.6 106.0 all-gather.1
where the time goes:
time: 253 us; the launch traced here: 251 us
  waiting for transfers between devices  159 us (63%)
  matrix products  43.9 us (17%)
  starting transfers between devices  28.9 us (11%)
  between operations  14.2 us (6%)
  local copies, waits for them, and re-layouts  3.96 us (2%)
    all_to_all x1, waiting for transfers between devices, local(): lax.all_to_all(send_rows, 'adapter', split_axis=0, concat_axis=0, tiled=T...  84.4 us
    all_to_all x1, waiting for transfers between devices, local(): lax.all_to_all(side, 'adapter', split_axis=0, concat_axis=0, tiled=True)  66.1 us
    dot_general x1, matrix products, local(): lax.dot_general(output_gradient, whole_weight, (((1,), (1,)), ((), ())),...  13.3 us
    dot_general x1, matrix products, local(): base_out = jnp.dot(tokens, whole_weight, preferred_element_type=jnp.float32)  8.1 us
    all_to_all x1, waiting for transfers between devices, local(): lax.all_to_all(send_grads, 'adapter', split_axis=0, concat_axis=0, tiled=...  7.9 us
    all_to_all x1, starting transfers between devices, local(): lax.all_to_all(side, 'adapter', split_axis=0, concat_axis=0, tiled=True)  7.86 us
    all_to_all x1, starting transfers between devices, local(): lax.all_to_all(send_rows, 'adapter', split_axis=0, concat_axis=0, tiled=T...  7.79 us
    all_to_all x1, starting transfers between devices, local(): lax.all_to_all(raised_rows, 'adapter', split_axis=0, concat_axis=0, tiled...  7.01 us
  transfers between devices with their start and end apart: 5, of which 3 were waited for; matrix products, arithmetic and copies ran while one was open for 19% of the time, Pallas kernels for 0%

commit v1 on v0

v1 whole, which is shorter than its diff:
```python
import functools

import jax
import jax.numpy as jnp
from jax import lax
from jax.experimental import pallas as pl
from jax.experimental.pallas import tpu as pltpu
from jax.sharding import PartitionSpec as P

adapter_scale = 2.0
NT = (((1,), (1,)), ((), ()))


def grid_sides(owners):
    ny = 1
    while (2 * ny) ** 2 <= owners:
        ny *= 2
    return owners // ny, ny


def exchange_kernel(
    nz, ny, rank, tile,
    idx_ref, a_ref, b_ref, x_ref, og_ref,
    a_all, b_all, x_all, og_all, lg_t, low_all, dg_own, dg_in, up_own, up_in,
    gbuf, rin, rin2, ubuf, uin, uin2, low_part, low_in, dg_out, up_out,
    loc_sem, ag_send, ag_recv, b_send, b_recv, y_send, y_recv,
    rs_send, rs_recv, rs_recv2, us_send, us_recv, us_recv2,
):
    me = lax.axis_index("adapter")
    z = me // ny
    y = lax.rem(me, ny)
    rows = a_ref.shape[1]
    width = a_ref.shape[2]
    vcols = ubuf.shape[2]
    owned = rows // rank

    def peer(d):
        return lax.rem(y + d, ny)

    def copy_to(src, dst, ssem, rsem, dev):
        return pltpu.make_async_remote_copy(
            src_ref=src, dst_ref=dst, send_sem=ssem, recv_sem=rsem,
            device_id={"adapter": dev}, device_id_type=pl.DeviceIdType.MESH,
        )

    barrier = pltpu.get_barrier_semaphore()

    def greet(dev):
        pl.semaphore_signal(
            barrier, inc=1, device_id={"adapter": dev}, device_id_type=pl.DeviceIdType.MESH
        )

    for d in range(1, ny):
        greet(z * ny + peer(d))
    pl.when(z > 0)(lambda: greet(me - ny))
    pl.when(z < nz - 1)(lambda: greet(me + ny))
    pl.semaphore_wait(
        barrier,
        (ny - 1) + jnp.where(z > 0, 1, 0) + jnp.where(z < nz - 1, 1, 0),
    )

    def y_copy(kind, d, src, dst):
        return copy_to(
            src, dst, y_send.at[kind, d - 1], y_recv.at[kind, d - 1], z * ny + peer(d)
        )

    def y_wait(kind, d, dst):
        copy_to(
            dst, dst, y_send.at[kind, d - 1], y_recv.at[kind, d - 1], z * ny + peer(ny - d)
        ).wait_recv()

    sends = []

    def y_start(kind, d, src, dst):
        c = y_copy(kind, d, src, dst)
        c.start()
        sends.append(c)

    for d in range(1, ny):
        y_start(0, d, b_ref, b_all.at[me])
    for d in range(1, ny):
        y_start(1, d, x_ref.at[peer(d)], x_all.at[y])
    for d in range(1, ny):
        y_start(2, d, a_ref.at[peer(d)], a_all.at[me])
    for d in range(1, ny):
        y_start(3, d, og_ref, og_all.at[y])
    local = [
        pltpu.make_async_copy(b_ref, b_all.at[me], loc_sem.at[0]),
        pltpu.make_async_copy(a_ref.at[y], a_all.at[me], loc_sem.at[1]),
        pltpu.make_async_copy(x_ref.at[y], x_all.at[y], loc_sem.at[2]),
        pltpu.make_async_copy(og_ref, og_all.at[y], loc_sem.at[3]),
    ]
    for c in local:
        c.start()
    for c in local:
        c.wait()

    def hop(buf, ssem, rsem, s, ys, last=False):
        n_left = (z - s) * ny + ys
        n_right = (z + s) * ny + ys

        def right(start):
            c = copy_to(buf.at[n_left], buf.at[n_left], ssem.at[0, n_left], rsem.at[n_left], me + ny)
            c.start() if start else c.wait_send()

        def left(start):
            c = copy_to(
                buf.at[n_right], buf.at[n_right], ssem.at[1, n_right], rsem.at[n_right], me - ny
            )
            c.start() if start else c.wait_send()

        if last:
            pl.when((z >= s) & (z < nz - 1))(lambda: right(False))
            pl.when((z + s < nz) & (z > 0))(lambda: left(False))
            return
        if s > 0:
            @pl.when(z >= s)
            def _():
                copy_to(
                    buf.at[n_left], buf.at[n_left], ssem.at[0, n_left], rsem.at[n_left], me - ny
                ).wait_recv()
        pl.when((z >= s) & (z < nz - 1))(lambda: right(True))
        if s > 0:
            @pl.when(z + s < nz)
            def _():
                copy_to(
                    buf.at[n_right], buf.at[n_right], ssem.at[1, n_right], rsem.at[n_right], me + ny
                ).wait_recv()
        pl.when((z + s < nz) & (z > 0))(lambda: left(True))

    for s in range(nz):
        hop(b_all, b_send, b_recv, s, y)
        if s == 0:
            hop(a_all, ag_send, ag_recv, s, y)
        for d in range(1, ny):
            if s == 0:
                y_wait(0, d, b_all.at[z * ny + peer(ny - d)])
            hop(b_all, b_send, b_recv, s, peer(ny - d))
        if s > 0:
            hop(a_all, ag_send, ag_recv, s, y)

    def masked(dense, n):
        adapter = n * owned + lax.broadcasted_iota(jnp.int32, dense.shape, 0) // rank
        return jnp.where(adapter == idx_ref[...], dense, 0.0).astype(jnp.bfloat16)

    def lg_block(n, carry):
        dense = adapter_scale * lax.dot_general(
            b_all[n], og_ref[...], NT, preferred_element_type=jnp.float32
        )
        lg_t[y, n] = masked(dense, n)
        return carry

    lax.fori_loop(0, nz * ny, lg_block, 0)
    for d in range(1, ny):
        y_start(4, d, lg_t.at[y], lg_t.at[y])
    for d in range(1, ny):
        y_wait(1, d, x_all.at[peer(ny - d)])
        y_wait(4, d, lg_t.at[peer(ny - d)])

    def grad(coef, acts, n, total, step, put, extra=()):
        @pl.loop(0, total // step)
        def _(i):
            cols = pl.ds(pl.multiple_of(i * step, step), step)
            acc = jnp.dot(coef[0, n], acts(0, cols), preferred_element_type=jnp.float32)
            for j in range(1, ny):
                acc += jnp.dot(coef[j, n], acts(j, cols), preferred_element_type=jnp.float32)
            for ref, at in extra:
                acc += ref[at, :, cols].astype(jnp.float32)
            put(cols, acc)

    def x_acts(j, cols):
        return x_all[j, :, cols]

    def v_acts(j, cols):
        return og_all[j, :, pl.ds(pl.multiple_of(y * vcols, vcols), vcols)]

    def reduce_step(t, coef, acts, out, inbox, inbox2, ssem, rsem, rsem2, total, step, last=False):
        for right in (True, False):
            pos = z if right else nz - 1 - z
            zo = (nz - 1 - (t - z)) if right else (t - (nz - 1 - z))
            ahead = me + ny if right else me - ny
            behind = me - ny if right else me + ny

            @pl.when((pos <= t) & (pos < nz - 1))
            def _():
                for yo in range(ny):
                    n = zo * ny + yo
                    if right:
                        c = copy_to(out.at[n], inbox.at[n], ssem.at[n], rsem.at[n], ahead)
                        c2 = None
                    else:
                        c = copy_to(out.at[n], inbox.at[n], ssem.at[n], rsem.at[n], ahead)
                        c2 = copy_to(out.at[n], inbox2.at[yo], ssem.at[n], rsem2.at[yo], ahead)
                    if last:
                        c.wait_send()
                        continue

                    def put(cols, acc):
                        out[n, :, cols] = acc.astype(jnp.bfloat16)

                    @pl.when(pos == 0)
                    def _():
                        grad(coef, acts, n, total, step, put)

                    @pl.when(pos > 0)
                    def _():
                        copy_to(inbox.at[n], inbox.at[n], ssem.at[n], rsem.at[n], behind).wait_recv()
                        grad(coef, acts, n, total, step, put, ((inbox, n),))

                    if right:
                        c.start()
                    else:
                        pl.when(zo == z - 1)(lambda: c2.start())
                        pl.when(zo < z - 1)(lambda: c.start())

    def reduce_end(coef, acts, own, out, kind, inbox, inbox2, rsem, rsem2, total, step):
        for d in range(ny):
            yo = lax.rem(y + d, ny)
            n = z * ny + yo

            @pl.when(z > 0)
            def _():
                copy_to(inbox.at[n], inbox.at[n], rsem.at[n], rsem.at[n], me - ny).wait_recv()

            @pl.when(z < nz - 1)
            def _():
                copy_to(
                    inbox2.at[yo], inbox2.at[yo], rsem2.at[yo], rsem2.at[yo], me + ny
                ).wait_recv()

            def put(cols, acc):
                if d == 0:
                    own[:, cols] = acc
                else:
                    out[d - 1, :, cols] = acc.astype(jnp.bfloat16)

            first, second = (inbox, n), (inbox2, yo)

            @pl.when((z > 0) & (z < nz - 1))
            def _():
                grad(coef, acts, n, total, step, put, (first, second))

            @pl.when(z == 0)
            def _():
                grad(coef, acts, n, total, step, put, (second,))

            @pl.when(z == nz - 1)
            def _():
                grad(coef, acts, n, total, step, put, (first,))

    def low_block(n):
        for j in range(ny):
            low_part[j, n] = lax.dot_general(
                a_all[n], x_all[j], NT, preferred_element_type=jnp.float32
            )

    down = (lg_t, x_acts, gbuf, rin, rin2, rs_send, rs_recv, rs_recv2, width, tile)
    for s in range(nz):
        for d in range(1, ny):
            if s == 0:
                y_wait(2, d, a_all.at[z * ny + peer(ny - d)])
            hop(a_all, ag_send, ag_recv, s, peer(ny - d))
        if s < nz - 1:
            reduce_step(s, *down)
        for yb in range(ny):
            pl.when(z >= s)(lambda: low_block((z - s) * ny + yb))
            if s > 0:
                pl.when(z + s < nz)(lambda: low_block((z + s) * ny + yb))

    for d in range(1, ny):
        y_start(5, d, low_part.at[peer(d)], low_in.at[d - 1])
    for d in range(1, ny):
        y_wait(5, d, low_in.at[d - 1])

    def low_sum(n, carry):
        total = low_part[y, n]
        for d in range(1, ny):
            total += low_in[d - 1, n]
        low_all[y, n] = masked(total, n)
        return carry

    lax.fori_loop(0, nz * ny, low_sum, 0)
    for d in range(1, ny):
        y_start(6, d, low_all.at[y], low_all.at[y])
    for d in range(1, ny):
        y_wait(3, d, og_all.at[peer(ny - d)])
        y_wait(6, d, low_all.at[peer(ny - d)])

    up = (low_all, v_acts, ubuf, uin, uin2, us_send, us_recv, us_recv2, vcols, vcols)
    for t in range(nz - 1):
        reduce_step(t, *up)
    reduce_end(lg_t, x_acts, dg_own, dg_out, 7, rin, rin2, rs_recv, rs_recv2, width, tile)
    for d in range(1, ny):
        y_start(7, d, dg_out.at[d - 1], dg_in.at[y])
    reduce_end(low_all, v_acts, up_own, up_out, 8, uin, uin2, us_recv, us_recv2, vcols, vcols)
    for d in range(1, ny):
        y_start(8, d, up_out.at[d - 1], up_in.at[y])
    dg_in[y] = jnp.zeros((rows, width), jnp.bfloat16)
    up_in[y] = jnp.zeros((rows, vcols), jnp.bfloat16)
    for d in range(1, ny):
        y_wait(7, d, dg_in.at[peer(ny - d)])
        y_wait(8, d, up_in.at[peer(ny - d)])

    for c in sends:
        c.wait_send()
    for s in range(nz):
        for d in range(ny):
            hop(b_all, b_send, b_recv, s, peer(d), last=True)
            hop(a_all, ag_send, ag_recv, s, peer(d), last=True)
    for t in range(nz - 1):
        reduce_step(t, *down, last=True)
        reduce_step(t, *up, last=True)


def exchange(nz, ny, rank, idx, a_cols, b_rows, x_cols, grads):
    nb = nz * ny
    _, rows, width = a_cols.shape
    tok_rows = x_cols.shape[1]
    kv_width = grads.shape[1]
    vcols = kv_width // ny
    bf, f32 = jnp.bfloat16, jnp.float32
    peers = max(1, ny - 1)
    outs = [
        ((nb, rows, width), bf),
        ((nb, rows, kv_width), bf),
        ((ny, tok_rows, width), bf),
        ((ny, tok_rows, kv_width), bf),
        ((ny, nb, rows, tok_rows), bf),
        ((ny, nb, rows, tok_rows), bf),
        ((rows, width), f32),
        ((ny, rows, width), bf),
        ((rows, vcols), f32),
        ((ny, rows, vcols), bf),
    ]
    vmem = pl.BlockSpec(memory_space=pltpu.VMEM)
    dma = pltpu.SemaphoreType.DMA
    return pl.pallas_call(
        functools.partial(exchange_kernel, nz, ny, rank, min(512, width)),
        out_shape=[jax.ShapeDtypeStruct(s, t) for s, t in outs],
        in_specs=[vmem] * 5,
        out_specs=[vmem] * len(outs),
        scratch_shapes=[
            pltpu.VMEM((nb, rows, width), bf),
            pltpu.VMEM((nb, rows, width), bf),
            pltpu.VMEM((ny, rows, width), bf),
            pltpu.VMEM((nb, rows, vcols), bf),
            pltpu.VMEM((nb, rows, vcols), bf),
            pltpu.VMEM((ny, rows, vcols), bf),
            pltpu.VMEM((ny, nb, rows, tok_rows), f32),
            pltpu.VMEM((peers, nb, rows, tok_rows), f32),
            pltpu.VMEM((peers, rows, width), bf),
            pltpu.VMEM((peers, rows, vcols), bf),
            dma((4,)),
            dma((2, nb)),
            dma((nb,)),
            dma((2, nb)),
            dma((nb,)),
            dma((9, peers)),
            dma((9, peers)),
            dma((nb,)),
            dma((nb,)),
            dma((ny,)),
            dma((nb,)),
            dma((nb,)),
            dma((ny,)),
        ],
        compiler_params=pltpu.CompilerParams(
            collective_id=0, has_side_effects=True, vmem_limit_bytes=60 * 1024 * 1024
        ),
    )(idx, a_cols, b_rows, x_cols, grads)


def local(
    tokens,
    token_adapter_index,
    frozen_value_weight,
    adapter_down_factors,
    adapter_up_factors,
    output_gradient,
):
    owners = lax.axis_size("adapter")
    shards = lax.axis_size("dp")
    nz, ny = grid_sides(owners)
    owned, rank, width = adapter_down_factors.shape
    tok_rows = tokens.shape[0]
    kv_width = output_gradient.shape[1]
    part = frozen_value_weight.shape[0] // ny
    y = lax.rem(lax.axis_index("adapter"), ny)

    def grouped(rows):
        return (
            rows.reshape(-1, shards, ny, part).transpose(2, 0, 1, 3).reshape(ny, -1, shards * part)
        )

    def joined(groups):
        return groups.reshape(ny, -1, shards, part).transpose(1, 2, 0, 3).reshape(-1, width)

    own_weight = lax.dynamic_slice_in_dim(frozen_value_weight, y * part, part, 0)
    weight = lax.all_gather(own_weight, "dp", axis=0, tiled=True)

    a_all, b_all, x_all, og_all, lg_t, low_all, dg_own, dg_in, up_own, up_in = exchange(
        nz, ny, rank,
        token_adapter_index.reshape(1, tok_rows),
        grouped(adapter_down_factors.reshape(owned * rank, width)),
        adapter_up_factors.reshape(owned * rank, kv_width),
        grouped(tokens),
        output_gradient,
    )
    slots = owners * owned * rank
    a_flat = a_all.reshape(slots, shards * part)
    pairs = {
        d: [(z * ny + i, z * ny + (i + d) % ny) for z in range(nz) for i in range(ny)]
        for d in range(1, ny)
    }

    def grads_of(j):
        lg = lax.dynamic_index_in_dim(lg_t, j, 0, False).reshape(slots, tok_rows)
        og = lax.dynamic_index_in_dim(og_all, j, 0, False)
        side = lax.dot_general(
            lg, a_flat, (((0,), (0,)), ((), ())), preferred_element_type=jnp.float32
        ).astype(jnp.bfloat16)
        back = lax.dot_general(
            og, weight, (((1,), (1,)), ((), ())), preferred_element_type=jnp.float32
        )
        return (back + side).astype(jnp.bfloat16)

    def base_of(j):
        x = lax.dynamic_index_in_dim(x_all, j, 0, False)
        return jnp.dot(x, weight, preferred_element_type=jnp.float32)

    grad_parts = jnp.zeros((ny, tok_rows, shards * part), jnp.bfloat16)
    base = base_of(y)
    for d in range(1, ny):
        to = lax.rem(y + d, ny)
        got = lax.ppermute(grads_of(to), "adapter", pairs[d])
        grad_parts = lax.dynamic_update_index_in_dim(grad_parts, got, lax.rem(y + ny - d, ny), 0)
        base += lax.ppermute(base_of(to).astype(jnp.bfloat16), "adapter", pairs[d]).astype(
            jnp.float32
        )
    grad_parts = lax.dynamic_update_index_in_dim(grad_parts, grads_of(y), y, 0)
    token_grad = joined(grad_parts)
    low_own = lax.dynamic_index_in_dim(low_all, y, 0, False).reshape(slots, tok_rows)
    lifted = (
        adapter_scale
        * lax.dot_general(
            low_own, b_all.reshape(slots, kv_width), (((0,), (0,)), ((), ())),
            preferred_element_type=jnp.float32,
        )
    ).astype(jnp.bfloat16)
    result = (base + lifted).astype(jnp.bfloat16)

    own = jnp.arange(ny)[:, None, None] == y
    down_grad = joined(jnp.where(own, dg_own[None], dg_in.astype(jnp.float32)))
    up_groups = adapter_scale * jnp.where(own, up_own[None], up_in.astype(jnp.float32))
    up_factor_gradient = up_groups.transpose(1, 0, 2).reshape(owned, rank, kv_width)
    return (result, token_grad, down_grad.reshape(owned, rank, width), up_factor_gradient)


def solution(mesh):
    in_specs = (
        P(("dp", "adapter"), None),
        P(("dp", "adapter"), None),
        P("dp", None),
        P(("dp", "adapter"), None, None),
        P(("dp", "adapter"), None, None),
        P(("dp", "adapter"), None),
    )
    out_specs = (
        P(("dp", "adapter"), None),
        P(("dp", "adapter"), None),
        P(("dp", "adapter"), None, None),
        P(("dp", "adapter"), None, None),
    )
    return jax.shard_map(local, mesh=mesh, in_specs=in_specs, out_specs=out_specs, check_vma=False)
```

time: 253 us -> 252 us (level)
  Pallas kernels: 0 us -> 168 us
  waiting for transfers between devices: 159 us -> 13.3 us
  local copies, waits for them, and re-layouts: 3.96 us -> 32.3 us
  starting transfers between devices: 28.9 us -> 1.11 us
  matrix products: 43.9 us -> 20.5 us
    pallas_call x0 -> x1, Pallas kernels: none -> 168 us  [exchange(): pl.pallas_call(functools.partial(exchange_kernel, nz, ny, rank, min(512,...]
    all_to_all x4 -> x0, waiting for transfers between devices: 158 us -> none  [the longest x1 84.4 us: local(): lax.all_to_all(send_rows, 'adapter', split_axis=0, concat_axis=0, tiled=T...]
    all_to_all x4 -> x0, starting transfers between devices: 28.9 us -> none  [the longest x1 7.86 us: local(): lax.all_to_all(side, 'adapter', split_axis=0, concat_axis=0, tiled=True)]
    dot_general x12 -> x7, matrix products: 43.9 us -> 20.5 us  [the longest x2 6.67 us: grads_of(): lax.dot_general(og, weight, (((1,), (1,)), ((), ())), preferred_element_t...]
    ppermute x0 -> x2, waiting for transfers between devices: none -> 13.3 us  [the longest x1 13.3 us: local(): got = lax.ppermute(grads_of(to), 'adapter', pairs[d])]
    reshape x0 -> x6, local copies, waits for them, and re-layouts: none -> 13.1 us  [the longest x4 9.78 us: grouped(): rows.reshape(-1, shards, ny, part).transpose(2, 0, 1, 3)]
    unnamed x14 -> x25, local copies, waits for them, and re-layouts: 0.87 us -> 5.35 us
    another operation x0 -> x3, local copies, waits for them, and re-layouts: none -> 3.99 us  [the longest x1 2.8 us: local(): down_grad.reshape(owned, rank, width)]
  transfers between devices with their start and end apart: 5 -> 3, of which waited for: 3 -> 1; matrix products, arithmetic and copies ran while one was open for 19% -> 15% of each run, Pallas kernels for 0% -> 67%
where the time goes in v1:
time: 252 us; the launch traced here: 251 us
  Pallas kernels  168 us (67%)
  local copies, waits for them, and re-layouts  32.3 us (13%)
  matrix products  20.5 us (8%)
  between operations  14.3 us (6%)
  waiting for transfers between devices  13.3 us (5%)
    pallas_call x1, Pallas kernels, exchange(): pl.pallas_call(functools.partial(exchange_kernel, nz, ny, rank, min(512,...  168 us
    ppermute x1, waiting for transfers between devices, local(): got = lax.ppermute(grads_of(to), 'adapter', pairs[d])  13.3 us
    reshape x4, local copies, waits for them, and re-layouts, grouped(): rows.reshape(-1, shards, ny, part).transpose(2, 0, 1, 3)  9.78 us
    dot_general x2, matrix products, grads_of(): lax.dot_general(og, weight, (((1,), (1,)), ((), ())), preferred_element_t...  6.67 us
    dot_general x2, matrix products, base_of(): return jnp.dot(x, weight, preferred_element_type=jnp.float32)  6.36 us
    unnamed x25, local copies, waits for them, and re-layouts  5.35 us
    dot_general x2, matrix products, grads_of(): lax.dot_general(lg, a_flat, (((0,), (0,)), ((), ())), preferred_element_t...  5.14 us
  transfers between devices with their start and end apart: 3, of which 1 were waited for; matrix products, arithmetic and copies ran while one was open for 15% of the time, Pallas kernels for 67%

profile of v1, /device:TPU:14, one launch (start us, length us, event | category | flops | bytes accessed | tf_op | source)
XLA Modules:
  0.0 251.1 jit_solution(18277445321857437320)
XLA Ops:
  7.2 0.0 all-gather.2.cloned.1.call-start
  7.2 3.1 %constant_dynamic-slice_fusion.3 = bf16[1024,1024]{1,0:T(8,128)(2,1)} fusion(bf16[2048,1024]{1,0:T(8,128)(2,1)} %param.8, s32[]{:T(128)S(6)} %select_n.29), kind=kLoop, calls=%fused_computation.35 | loop fusion | bytes 4194308 | tf_op jit(solution)/shard_map/dynamic_slice | solution.py:398
  10.3 0.0 copy-start.4
  10.3 0.0 all-gather.2.cloned.1.call-update
  10.3 1.2 copy-done.4
  11.5 0.8 reshape_reshape.6
  12.3 0.4 copy.30
  12.7 0.0 copy-start.3
  12.7 1.6 reshape.61.a_ref
  14.4 0.2 copy-done.3
  14.5 2.7 %reshape.63 = bf16[128,4,2,1024]{3,2,1,0:T(2,128)(2,1)} reshape(bf16[128,8192]{1,0:T(8,128)(2,1)S(1)} %copy-done.3) | data formatting | bytes 4194304 | tf_op jit(solution)/shard_map/reshape | solution.py:392
  17.2 2.7 %copy.29 = bf16[128,4,2,1024]{3,1,0,2:T(4,128)(2,1)S(1)} copy(bf16[128,4,2,1024]{3,2,1,0:T(2,128)(2,1)} %reshape.63) | data formatting | bytes 4194304 | tf_op jit(solution)/shard_map/reshape | solution.py:392
  19.9 2.8 %reshape.64.x_ref = bf16[2,128,4096]{2,1,0:T(8,128)(2,1)} reshape(bf16[2,128,4,1024]{3,2,1,0:T(4,128)(2,1)S(1)} %bitcast.50) | data formatting | bytes 4194304 | tf_op jit(solution)/shard_map/reshape | solution.py:392
  22.7 167.7 %shard_map.93 = (bf16[8,64,4096]{2,1,0:T(8,128)(2,1)}, bf16[8,64,1024]{2,1,0:T(8,128)(2,1)}, bf16[2,128,4096]{2,1,0:T(8,128)(2,1)}, bf16[2,128,1024]{2,1,0:T(8,1...) custom-call(s32[1,128]{1,0:T(1,128)} %bitcast.59, ...), custom_call_target="tpu_custom_call" | custom-call | tf_op jit(solution)/shard_map/pallas_call | solution.py:337
  190.4 1.8 convert_select_fusion
  192.3 2.4 reshape.72
  194.7 3.5 %copy.24 = f32[64,4,2,1024]{3,2,1,0:T(2,128)S(1)} copy(f32[64,4,2,1024]{3,1,0,2:T(4,128)} %bitcast.51) | data formatting | bytes 4194304 | tf_op jit(solution)/shard_map/transpose | solution.py:396
  198.2 0.0 copy-start.7
  198.2 0.0 copy-start.8
  198.2 0.0 copy-start.9
  198.2 0.0 copy-start.6
  198.2 2.8 %reshape_reshape.7 = f32[4,16,8192]{2,1,0:T(8,128)} reshape(f32[64,4,2,1024]{3,2,1,0:T(2,128)S(1)} %copy.24) | data formatting | bytes 4194304 | tf_op jit(solution)/shard_map/reshape;reshape | solution.py:456
  201.0 0.0 copy-done.7
  201.0 0.0 copy-done.8
  201.0 0.1 multiply_bitcast_fusion
  201.1 0.2 copy.25
  201.3 0.9 reshape.73
  202.3 0.0 copy-done.9
  202.3 0.0 copy-done.6
  202.3 0.0 copy-start
  202.3 4.4 %fusion.3 = f32[128,4096]{1,0:T(8,128)} fusion(bf16[512,128]{1,0:T(8,128)(2,1)S(1)} %bitcast.57, bf16[512,4096]{1,0:T(8,128)(2,1)} %bitcast.47), kind=kOutput, calls=%fused_computation.7 | convolution fusion | flops 537919488 | bytes 6422528 | tf_op jit(solution)/shard_map/dot_general | solution.py:419
  206.7 0.0 copy-done
  206.7 0.7 fusion.2
  207.5 0.0 all-gather.2.cloned.1.call-done
  207.5 0.0 slice-start
  207.5 0.0 slice-start.1
  207.5 0.0 copy-start.1
  207.5 0.0 copy-start.5
  207.6 5.1 %convolution_convert_fusion.2 = bf16[128,1024]{1,0:T(8,128)(2,1)S(1)} fusion(bf16[4096,1024]{1,0:T(8,128)(2,1)} %all-gather.2.cloned.1.call-done, bf16[2,128,4096]{2,1,0:T(8,128)(2,1)} %get-tuple-element.14, s32[]{:T(128)S(6)} %select_n.30), kind=kOutput, calls=%fused_computation.14 | convolution fusion | flops 1073872896 | bytes 9699332 | tf_op jit(solution)/shard_map/dot_general | solution.py:429
  212.7 0.6 collective-permute-start
  213.2 0.0 slice-done
  213.2 0.4 slice-done.1
  213.7 0.6 copy-done.1
  214.3 0.0 copy-done.5
  214.3 3.8 %fusion = bf16[128,4096]{1,0:T(8,128)(2,1)} fusion(f32[128,4096]{1,0:T(8,128)S(1)} %copy-done.1, bf16[4096,1024]{1,0:T(8,128)(2,1)S(1)} %bitcast.46, bf16[2,128,1024]{2,1,0:T(8,128)(2,1)S(1)} %copy-done.5, s32[]{:T(128)S(6)} %select_n.30), kind=kOutput, calls=%fused_computation.2 | convolution fusion | flops 1074790400 | bytes 11796484 | tf_op jit(solution)/shard_map/dot_general | solution.py:422
  218.1 0.0 copy-start.2
  218.1 0.5 collective-permute-start.1
  218.6 2.9 %fusion.4 = bf16[1,128,4096]{2,1,0:T(8,128)(2,1)S(1)} fusion(f32[128,4096]{1,0:T(8,128)S(1)} %fusion.2, bf16[4096,1024]{1,0:T(8,128)(2,1)S(1)} %bitcast.46, bf16[2,128,1024]{2,1,0:T(8,128)(2,1)S(1)} %copy-done.5, s32[]{:T(128)S(6)} %select_n.28), kind=kOutput, calls=%fused_computation.8 | convolution fusion | flops 1074790400 | bytes 11796484 | tf_op jit(solution)/shard_map/dot_general | solution.py:422
  221.5 0.0 copy-done.2
  221.5 1.3 fusion.8
  222.8 0.7 copy.22
  223.4 0.0 collective-permute-done
  223.5 2.3 add_convert_fusion
  225.8 13.3 %collective-permute-done.1 = bf16[128,4096]{1,0:T(8,128)(2,1)} collective-permute-done((bf16[128,4096]{1,0:T(8,128)(2,1)}, bf16[128,4096]{1,0:T(8,128)(2,1)}, u32[]{:S(2)}, u32[]{:S(2)}) %collective-permute-start.1) | collective-permute-done | bytes 1048608 | tf_op jit(solution)/shard_map/ppermute | solution.py:435
  239.0 1.6 copy.21
  240.7 0.3 broadcast_in_dim.45
  240.9 0.1 constant_dynamic-update-slice_fusion.1
  241.1 0.1 constant_dynamic-update-slice_fusion
  241.2 0.1 copy.23
  241.4 2.9 %copy.26 = bf16[128,8192]{1,0:T(8,128)(2,1)} copy(bf16[128,8192]{0,1:T(8,128)(2,1)S(1)} %bitcast.52) | data formatting | bytes 4194304
  (4 shorter events, 0.0 us)
Async XLA Ops:
  7.2 200.3 %all-gather.2.cloned.1.call-start = ((), (), s32[]{:S(2)}) async-start(), calls=%async_computation | async-start | bytes 10485760 | tf_op jit(solution)/shard_map/all_gather | solution.py:399
  10.3 1.2 copy-start.4
  12.7 1.8 copy-start.3
  198.2 2.8 %copy-start.7 = (f32[64,512]{1,0:T(8,128)S(1)}, f32[64,512]{1,0:T(8,128)}, u32[]{:S(2)}) copy-start(f32[64,512]{1,0:T(8,128)} %get-tuple-element.22) | copy-start | bytes 393220
  198.2 2.8 %copy-start.8 = (bf16[2,64,512]{2,1,0:T(8,128)(2,1)S(1)}, bf16[2,64,512]{2,1,0:T(8,128)(2,1)}, u32[]{:S(2)}) copy-start(bf16[2,64,512]{2,1,0:T(8,128)(2,1)} %get-tuple-element.23) | copy-start | bytes 393220
  198.2 4.1 %copy-start.9 = (bf16[2,8,64,128]{3,2,1,0:T(8,128)(2,1)S(1)}, bf16[2,8,64,128]{3,2,1,0:T(8,128)(2,1)}, u32[]{:S(2)}) copy-start(bf16[2,8,64,128]{3,2,1,0:T(8,128)(2,1)} %get-tuple-element.15) | copy-start | bytes 786436
  198.2 4.1 %copy-start.6 = (bf16[2,8,64,128]{3,2,1,0:T(8,128)(2,1)S(1)}, bf16[2,8,64,128]{3,2,1,0:T(8,128)(2,1)}, u32[]{:S(2)}) copy-start(bf16[2,8,64,128]{3,2,1,0:T(8,128)(2,1)} %get-tuple-element.18) | copy-start | bytes 786436
  202.3 4.4 %copy-start = (bf16[8,64,4096]{2,1,0:T(8,128)(2,1)S(1)}, bf16[8,64,4096]{2,1,0:T(8,128)(2,1)}, u32[]{:S(2)}) copy-start(bf16[8,64,4096]{2,1,0:T(8,128)(2,1)} %get-tuple-element.19) | copy-start | bytes 12582916
  207.5 5.7 %slice-start = ((s8[8388608]{0:T(1024)(128)(4,1)}), s8[4194304]{0:T(1024)(128)(4,1)S(1)}, s32[]{:S(2)}) async-start(s8[8388608]{0:T(1024)(128)(4,1)} %bitcast.45), calls=%async_computation.1 | async-start | bytes 8388608
  207.5 6.2 %slice-start.1 = ((s8[8388608]{0:T(1024)(128)(4,1)}), s8[4194304]{0:T(1024)(128)(4,1)S(1)}, s32[]{:S(2)}) async-start(s8[8388608]{0:T(1024)(128)(4,1)} %bitcast.45), calls=%async_computation.2 | async-start | bytes 8388608
  207.5 6.7 %copy-start.1 = (f32[128,4096]{1,0:T(8,128)S(1)}, f32[128,4096]{1,0:T(8,128)}, u32[]{:S(2)}) copy-start(f32[128,4096]{1,0:T(8,128)} %fusion.3) | copy-start | bytes 6291460
  207.5 6.8 %copy-start.5 = (bf16[2,128,1024]{2,1,0:T(8,128)(2,1)S(1)}, bf16[2,128,1024]{2,1,0:T(8,128)(2,1)}, u32[]{:S(2)}) copy-start(bf16[2,128,1024]{2,1,0:T(8,128)(2,1)} %get-tuple-element.17) | copy-start | bytes 1572868
  212.7 10.8 %collective-permute-start = (bf16[128,1024]{1,0:T(8,128)(2,1)S(1)}, bf16[128,1024]{1,0:T(8,128)(2,1)}, u32[]{:S(2)}, u32[]{:S(2)}) collective-permute-start(bf16[128,1024]{1,0:T(8,128)(2,1)S(1)} %convolution_convert_fusion.2), channel_id=1, source_target_pairs={{0,1},{1,0},{2,3},{3,2},{4,5},{5,4},{6,7},{7,6},{8,9},{9,8},{10,11... | collective-permute-start | bytes 786440 | tf_op jit(solution)/shard_map/ppermute | solution.py:437
  218.1 3.4 %copy-start.2 = (bf16[2,128,4096]{2,1,0:T(8,128)(2,1)S(1)}, bf16[2,128,4096]{2,1,0:T(8,128)(2,1)}, u32[]{:S(2)}) copy-start(bf16[2,128,4096]{2,1,0:T(8,128)(2,1)} %get-tuple-element.14) | copy-start | bytes 6291460
  218.1 20.9 %collective-permute-start.1 = (bf16[128,4096]{1,0:T(8,128)(2,1)}, bf16[128,4096]{1,0:T(8,128)(2,1)}, u32[]{:S(2)}, u32[]{:S(2)}) collective-permute-start(bf16[128,4096]{1,0:T(8,128)(2,1)} %fusion), channel_id=1, source_target_pairs={{0,1},{1,0},{2,3},{3,2},{4,5},{5,4},{6,7},{7,6},{8,9},{9,8},{10,11... | collective-permute-start | bytes 3145736 | tf_op jit(solution)/shard_map/ppermute | solution.py:435
Sparse Core Ops, SparseCore 0:
  10.5 58.4 all-gather.1

commit v2 on v1

v2 whole, which is shorter than its diff:
```python
import functools

import jax
import jax.numpy as jnp
from jax import lax
from jax.experimental import pallas as pl
from jax.experimental.pallas import tpu as pltpu
from jax.sharding import PartitionSpec as P

adapter_scale = 2.0
NT = (((1,), (1,)), ((), ()))


def grid_sides(owners):
    ny = 1
    while (2 * ny) ** 2 <= owners:
        ny *= 2
    return owners // ny, ny


def exchange_kernel(
    nz, ny, rank, shards, tile,
    idx_ref, a_ref, b_ref, x_ref, og_ref,
    a_all, b_all, x_all, og_all, lg_t, low_all, dg_full, up_full,
    gbuf, rin, rin2, ubuf, uin, uin2, low_part, low_in, dg_out, dg_in, up_out, up_in,
    loc_sem, ag_send, ag_recv, b_send, b_recv, y_send, y_recv,
    rs_send, rs_recv, rs_recv2, us_send, us_recv, us_recv2,
):
    me = lax.axis_index("adapter")
    z = me // ny
    y = lax.rem(me, ny)
    rows, width = a_all.shape[1:]
    tok = og_ref.shape[0]
    part = width // shards
    vcols = ubuf.shape[2]
    owned = rows // rank
    nb = nz * ny

    def peer(d):
        return lax.rem(y + d, ny)

    def back(d):
        return lax.rem(y + ny - d, ny)

    def slot(j):
        return pl.ds(pl.multiple_of(j * tok, tok), tok)

    def copy_to(src, dst, ssem, rsem, dev):
        return pltpu.make_async_remote_copy(
            src_ref=src, dst_ref=dst, send_sem=ssem, recv_sem=rsem,
            device_id={"adapter": dev}, device_id_type=pl.DeviceIdType.MESH,
        )

    barrier = pltpu.get_barrier_semaphore()

    def greet(dev):
        pl.semaphore_signal(
            barrier, inc=1, device_id={"adapter": dev}, device_id_type=pl.DeviceIdType.MESH
        )

    for d in range(1, ny):
        greet(z * ny + peer(d))
    pl.when(z > 0)(lambda: greet(me - ny))
    pl.when(z < nz - 1)(lambda: greet(me + ny))
    pl.semaphore_wait(
        barrier,
        (ny - 1) + jnp.where(z > 0, 1, 0) + jnp.where(z < nz - 1, 1, 0),
    )

    sends = []

    def y_start(kind, d, src, dst):
        c = copy_to(
            src, dst, y_send.at[kind, d - 1], y_recv.at[kind, d - 1], z * ny + peer(d)
        )
        c.start()
        sends.append(c)

    def pieces(src, j, dst):
        for q in range(shards):
            at = pl.ds(pl.multiple_of((q * ny + j) * part, part), part)
            yield src.at[:, at], dst.at[:, pl.ds(q * part, part)]

    def y_start_columns(kind, d, src, dst):
        ssem, rsem, dev = y_send.at[kind, d - 1], y_recv.at[kind, d - 1], z * ny + peer(d)
        for piece, to in pieces(src, peer(d), dst):
            copy_to(piece, to, ssem, rsem, dev).start()
        sends.append(copy_to(dst, dst, ssem, rsem, dev))

    def y_wait(kind, d, dst):
        copy_to(
            dst, dst, y_send.at[kind, d - 1], y_recv.at[kind, d - 1], z * ny + back(d)
        ).wait_recv()

    for d in range(1, ny):
        y_start(0, d, b_ref, b_all.at[me])
    for d in range(1, ny):
        y_start_columns(1, d, x_ref, x_all.at[slot(y)])
    keep_b = pltpu.make_async_copy(b_ref, b_all.at[me], loc_sem.at[0])
    keep_og = pltpu.make_async_copy(og_ref, og_all.at[slot(y)], loc_sem.at[3])
    keep_b.start()
    for src, dst in pieces(a_ref, y, a_all.at[me]):
        pltpu.make_async_copy(src, dst, loc_sem.at[1]).start()
    for src, dst in pieces(x_ref, y, x_all.at[slot(y)]):
        pltpu.make_async_copy(src, dst, loc_sem.at[2]).start()
    keep_og.start()

    def hop(buf, ssem, rsem, s, ys, last=False):
        n_left = (z - s) * ny + ys
        n_right = (z + s) * ny + ys

        def right(start):
            c = copy_to(buf.at[n_left], buf.at[n_left], ssem.at[0, n_left], rsem.at[n_left], me + ny)
            c.start() if start else c.wait_send()

        def left(start):
            c = copy_to(
                buf.at[n_right], buf.at[n_right], ssem.at[1, n_right], rsem.at[n_right], me - ny
            )
            c.start() if start else c.wait_send()

        if last:
            pl.when((z >= s) & (z < nz - 1))(lambda: right(False))
            pl.when((z + s < nz) & (z > 0))(lambda: left(False))
            return
        if s > 0:
            @pl.when(z >= s)
            def _():
                copy_to(
                    buf.at[n_left], buf.at[n_left], ssem.at[0, n_left], rsem.at[n_left], me - ny
                ).wait_recv()
        pl.when((z >= s) & (z < nz - 1))(lambda: right(True))
        if s > 0:
            @pl.when(z + s < nz)
            def _():
                copy_to(
                    buf.at[n_right], buf.at[n_right], ssem.at[1, n_right], rsem.at[n_right], me + ny
                ).wait_recv()
        pl.when((z + s < nz) & (z > 0))(lambda: left(True))

    def hop_b(s):
        hop(b_all, b_send, b_recv, s, y)
        for d in range(1, ny):
            if s == 0:
                y_wait(0, d, b_all.at[z * ny + back(d)])
            hop(b_all, b_send, b_recv, s, back(d))

    def hop_own(s):
        hop(a_all, ag_send, ag_recv, s, y)

    def hop_peers(s):
        for d in range(1, ny):
            if s == 0:
                y_wait(2, d, a_all.at[z * ny + back(d)])
            hop(a_all, ag_send, ag_recv, s, back(d))

    keep_b.wait()
    hop_b(0)
    pltpu.make_async_copy(a_all.at[me], a_all.at[me], loc_sem.at[1]).wait()
    hop_own(0)
    hop_b(1)
    for s in range(2, nz):
        hop_b(s)
        if s < nz - 1:
            hop_own(s - 1)

    def masked(dense, n):
        adapter = n * owned + lax.broadcasted_iota(jnp.int32, dense.shape, 0) // rank
        return jnp.where(adapter == idx_ref[...], dense, 0.0).astype(jnp.bfloat16)

    def lg_block(n, carry):
        dense = adapter_scale * lax.dot_general(
            b_all[n], og_ref[...], NT, preferred_element_type=jnp.float32
        )
        lg_t[n, :, slot(y)] = masked(dense, n)
        return carry

    lax.fori_loop(0, nb, lg_block, 0)
    for d in range(1, ny):
        y_start(4, d, lg_t.at[:, :, slot(y)], lg_t.at[:, :, slot(y)])
    for d in range(1, ny):
        y_start_columns(2, d, a_ref, a_all.at[me])
    keep_og.wait()
    for d in range(1, ny):
        y_start(3, d, og_ref, og_all.at[slot(y)])
    pltpu.make_async_copy(x_all.at[slot(y)], x_all.at[slot(y)], loc_sem.at[2]).wait()
    for d in range(1, ny):
        y_wait(1, d, x_all.at[slot(back(d))])
        y_wait(4, d, lg_t.at[:, :, slot(back(d))])

    def grad(coef, acts, n, count, total, step, put, extra=()):
        blocks = pl.ds(n, count)

        @pl.loop(0, total // step)
        def _(i):
            start = pl.multiple_of(i * step, step)
            cols = pl.ds(start, step)
            acc = jnp.dot(
                coef[blocks].reshape(count * rows, coef.shape[2]), acts(cols),
                preferred_element_type=jnp.float32,
            )
            for ref, at in extra:
                acc += ref[pl.ds(at, count), :, cols].reshape(count * rows, step).astype(
                    jnp.float32
                )
            put(start, cols, acc)

    def x_acts(cols):
        return x_all[:, cols]

    def v_acts(cols):
        return og_all[:, pl.ds(pl.multiple_of(y * vcols, vcols), vcols)]

    def reduce_step(t, coef, acts, out, inbox, inbox2, ssem, rsem, rsem2, total, step, last=False):
        for right in (True, False):
            pos = z if right else nz - 1 - z
            zo = (nz - 1 - (t - z)) if right else (t - (nz - 1 - z))
            ahead = me + ny if right else me - ny
            behind = me - ny if right else me + ny

            @pl.when((pos <= t) & (pos < nz - 1))
            def _():
                blocks = pl.ds(zo * ny, ny)

                def send(dst, recv):
                    return copy_to(out.at[blocks], dst, ssem.at[zo], recv, ahead)

                if last:
                    send(inbox.at[blocks], rsem.at[zo]).wait_send()
                    return

                def put(start, cols, acc):
                    out[blocks, :, cols] = acc.astype(jnp.bfloat16).reshape(ny, rows, step)

                @pl.when(pos == 0)
                def _():
                    grad(coef, acts, zo * ny, ny, total, step, put)

                @pl.when(pos > 0)
                def _():
                    copy_to(
                        inbox.at[blocks], inbox.at[blocks], ssem.at[zo], rsem.at[zo], behind
                    ).wait_recv()
                    grad(coef, acts, zo * ny, ny, total, step, put, ((inbox, zo * ny),))

                if right:
                    send(inbox.at[blocks], rsem.at[zo]).start()
                else:
                    pl.when(zo == z - 1)(lambda: send(inbox2, rsem2.at[0]).start())
                    pl.when(zo < z - 1)(lambda: send(inbox.at[blocks], rsem.at[zo]).start())

    def reduce_end(coef, acts, own, out, inbox, inbox2, rsem, rsem2, total, step):
        blocks = pl.ds(z * ny, ny)

        @pl.when(z > 0)
        def _():
            copy_to(inbox.at[blocks], inbox.at[blocks], rsem.at[z], rsem.at[z], me - ny).wait_recv()

        @pl.when(z < nz - 1)
        def _():
            copy_to(inbox2, inbox2, rsem2.at[0], rsem2.at[0], me + ny).wait_recv()

        for d in range(1, ny + 1):
            yo = lax.rem(y + d, ny)
            n = z * ny + yo

            def put(start, cols, acc):
                if d == ny:
                    own(y, start, acc)
                else:
                    out[d - 1, :, cols] = acc.astype(jnp.bfloat16)

            first, second = (inbox, n), (inbox2, yo)

            @pl.when((z > 0) & (z < nz - 1))
            def _():
                grad(coef, acts, n, 1, total, step, put, (first, second))

            @pl.when(z == 0)
            def _():
                grad(coef, acts, n, 1, total, step, put, (second,))

            @pl.when(z == nz - 1)
            def _():
                grad(coef, acts, n, 1, total, step, put, (first,))

            yield d

    def down_at(j, start, values):
        q = start // part
        at = pl.multiple_of((q * ny + j) * part + start - q * part, tile)
        dg_full[:, pl.ds(at, tile)] = values

    def up_at(j, start, values):
        up_full[:, pl.ds(pl.multiple_of(j * vcols, vcols), vcols)] = adapter_scale * values

    down = (lg_t, x_acts, gbuf, rin, rin2, rs_send, rs_recv, rs_recv2, width, tile)
    up = (low_all, v_acts, ubuf, uin, uin2, us_send, us_recv, us_recv2, vcols, vcols)
    reduce_step(0, *down)
    if nz > 2:
        hop_own(nz - 2)
    hop_peers(0)
    for s in range(1, nz - 1):
        hop_peers(s)
        reduce_step(s, *down)
    hop_own(nz - 1)
    hop_peers(nz - 1)

    for j in range(ny):
        low_part[j] = jnp.zeros((nb * rows, tok), jnp.float32)

        @pl.loop(0, width // tile)
        def _(i):
            cols = pl.ds(pl.multiple_of(i * tile, tile), tile)
            low_part[j] += lax.dot_general(
                a_all[:, :, cols].reshape(nb * rows, tile), x_all[slot(j), cols], NT,
                preferred_element_type=jnp.float32,
            )

    for d in range(1, ny):
        y_start(5, d, low_part.at[peer(d)], low_in.at[d - 1])
    for d in range(1, ny):
        y_wait(5, d, low_in.at[d - 1])

    def low_sum(n, carry):
        at = pl.ds(pl.multiple_of(n * rows, rows), rows)
        total = low_part[y, at]
        for d in range(1, ny):
            total += low_in[d - 1, at]
        low_all[n, :, slot(y)] = masked(total, n)
        return carry

    lax.fori_loop(0, nb, low_sum, 0)
    for d in range(1, ny):
        y_start(6, d, low_all.at[:, :, slot(y)], low_all.at[:, :, slot(y)])
    for d in range(1, ny):
        y_wait(3, d, og_all.at[slot(back(d))])
        y_wait(6, d, low_all.at[:, :, slot(back(d))])

    for t in range(nz - 1):
        reduce_step(t, *up)
    for d in reduce_end(
        lg_t, x_acts, down_at, dg_out, rin, rin2, rs_recv, rs_recv2, width, tile
    ):
        if d < ny:
            y_start(7, d, dg_out.at[d - 1], dg_in.at[d - 1])
    for d in reduce_end(
        low_all, v_acts, up_at, up_out, uin, uin2, us_recv, us_recv2, vcols, vcols
    ):
        if d < ny:
            y_start(8, d, up_out.at[d - 1], up_in.at[d - 1])
    for d in range(1, ny):
        y_wait(8, d, up_in.at[d - 1])
        up_at(back(d), 0, up_in[d - 1].astype(jnp.float32))
    for d in range(1, ny):
        y_wait(7, d, dg_in.at[d - 1])

        @pl.loop(0, width // tile)
        def _(i):
            start = pl.multiple_of(i * tile, tile)
            down_at(back(d), start, dg_in[d - 1, :, pl.ds(start, tile)].astype(jnp.float32))

    for c in sends:
        c.wait_send()
    for s in range(nz):
        for d in range(ny):
            hop(b_all, b_send, b_recv, s, peer(d), last=True)
            hop(a_all, ag_send, ag_recv, s, peer(d), last=True)
    for t in range(nz - 1):
        reduce_step(t, *down, last=True)
        reduce_step(t, *up, last=True)


def exchange(nz, ny, shards, rank, idx, a_rows, b_rows, tokens, grads):
    nb = nz * ny
    rows = a_rows.shape[0]
    width = a_rows.shape[1] // ny
    tok_rows = tokens.shape[0]
    kv_width = grads.shape[1]
    vcols = kv_width // ny
    bf, f32 = jnp.bfloat16, jnp.float32
    peers = max(1, ny - 1)
    outs = [
        ((nb, rows, width), bf),
        ((nb, rows, kv_width), bf),
        ((ny * tok_rows, width), bf),
        ((ny * tok_rows, kv_width), bf),
        ((nb, rows, ny * tok_rows), bf),
        ((nb, rows, ny * tok_rows), bf),
        ((rows, ny * width), f32),
        ((rows, kv_width), f32),
    ]
    vmem = pl.BlockSpec(memory_space=pltpu.VMEM)
    dma = pltpu.SemaphoreType.DMA
    return pl.pallas_call(
        functools.partial(
            exchange_kernel, nz, ny, rank, shards, min(512, width // shards)
        ),
        out_shape=[jax.ShapeDtypeStruct(s, t) for s, t in outs],
        in_specs=[vmem] * 5,
        out_specs=[vmem] * len(outs),
        scratch_shapes=[
            pltpu.VMEM((nb, rows, width), bf),
            pltpu.VMEM((nb, rows, width), bf),
            pltpu.VMEM((ny, rows, width), bf),
            pltpu.VMEM((nb, rows, vcols), bf),
            pltpu.VMEM((nb, rows, vcols), bf),
            pltpu.VMEM((ny, rows, vcols), bf),
            pltpu.VMEM((ny, nb * rows, tok_rows), f32),
            pltpu.VMEM((peers, nb * rows, tok_rows), f32),
            pltpu.VMEM((peers, rows, width), bf),
            pltpu.VMEM((peers, rows, width), bf),
            pltpu.VMEM((peers, rows, vcols), bf),
            pltpu.VMEM((peers, rows, vcols), bf),
            dma((4,)),
            dma((2, nb)),
            dma((nb,)),
            dma((2, nb)),
            dma((nb,)),
            dma((9, peers)),
            dma((9, peers)),
            dma((nz,)),
            dma((nz,)),
            dma((1,)),
            dma((nz,)),
            dma((nz,)),
            dma((1,)),
        ],
        compiler_params=pltpu.CompilerParams(
            collective_id=0, has_side_effects=True, vmem_limit_bytes=60 * 1024 * 1024
        ),
    )(idx, a_rows, b_rows, tokens, grads)


def local(
    tokens,
    token_adapter_index,
    frozen_value_weight,
    adapter_down_factors,
    adapter_up_factors,
    output_gradient,
):
    owners = lax.axis_size("adapter")
    shards = lax.axis_size("dp")
    nz, ny = grid_sides(owners)
    owned, rank, width = adapter_down_factors.shape
    tok_rows = tokens.shape[0]
    kv_width = output_gradient.shape[1]
    part = frozen_value_weight.shape[0] // ny
    y = lax.rem(lax.axis_index("adapter"), ny)

    def joined(groups):
        return groups.reshape(ny, -1, shards, part).transpose(1, 2, 0, 3).reshape(-1, width)

    own_weight = lax.dynamic_slice_in_dim(frozen_value_weight, y * part, part, 0)
    weight = lax.all_gather(own_weight, "dp", axis=0, tiled=True)

    a_all, b_all, x_all, og_all, lg_t, low_all, down_grad, up_factor_gradient = exchange(
        nz, ny, shards, rank,
        token_adapter_index.reshape(1, tok_rows),
        adapter_down_factors.reshape(owned * rank, width),
        adapter_up_factors.reshape(owned * rank, kv_width),
        tokens,
        output_gradient,
    )
    slots = owners * owned * rank
    a_flat = a_all.reshape(slots, shards * part)
    pairs = {
        d: [(z * ny + i, z * ny + (i + d) % ny) for z in range(nz) for i in range(ny)]
        for d in range(1, ny)
    }

    def grads_of(j):
        lg = lax.dynamic_slice_in_dim(
            lg_t.reshape(slots, ny * tok_rows), j * tok_rows, tok_rows, 1
        )
        og = lax.dynamic_slice_in_dim(og_all, j * tok_rows, tok_rows, 0)
        side = lax.dot_general(
            lg, a_flat, (((0,), (0,)), ((), ())), preferred_element_type=jnp.float32
        ).astype(jnp.bfloat16)
        back = lax.dot_general(
            og, weight, (((1,), (1,)), ((), ())), preferred_element_type=jnp.float32
        )
        return (back + side).astype(jnp.bfloat16)

    def base_of(j):
        x = lax.dynamic_slice_in_dim(x_all, j * tok_rows, tok_rows, 0)
        return jnp.dot(x, weight, preferred_element_type=jnp.float32)

    grad_parts = jnp.zeros((ny, tok_rows, shards * part), jnp.bfloat16)
    base = base_of(y)
    for d in range(1, ny):
        to = lax.rem(y + d, ny)
        got = lax.ppermute(grads_of(to), "adapter", pairs[d])
        grad_parts = lax.dynamic_update_index_in_dim(grad_parts, got, lax.rem(y + ny - d, ny), 0)
        base += lax.ppermute(base_of(to).astype(jnp.bfloat16), "adapter", pairs[d]).astype(
            jnp.float32
        )
    grad_parts = lax.dynamic_update_index_in_dim(grad_parts, grads_of(y), y, 0)
    token_grad = joined(grad_parts)
    low_own = lax.dynamic_slice_in_dim(
        low_all.reshape(slots, ny * tok_rows), y * tok_rows, tok_rows, 1
    )
    lifted = (
        adapter_scale
        * lax.dot_general(
            low_own, b_all.reshape(slots, kv_width), (((0,), (0,)), ((), ())),
            preferred_element_type=jnp.float32,
        )
    ).astype(jnp.bfloat16)
    result = (base + lifted).astype(jnp.bfloat16)

    return (
        result,
        token_grad,
        down_grad.reshape(owned, rank, width),
        up_factor_gradient.reshape(owned, rank, kv_width),
    )


def solution(mesh):
    in_specs = (
        P(("dp", "adapter"), None),
        P(("dp", "adapter"), None),
        P("dp", None),
        P(("dp", "adapter"), None, None),
        P(("dp", "adapter"), None, None),
        P(("dp", "adapter"), None),
    )
    out_specs = (
        P(("dp", "adapter"), None),
        P(("dp", "adapter"), None),
        P(("dp", "adapter"), None, None),
        P(("dp", "adapter"), None, None),
    )
    return jax.shard_map(local, mesh=mesh, in_specs=in_specs, out_specs=out_specs, check_vma=False)
```

time: 252 us -> 207 us (0.82)
  Pallas kernels: 168 us -> 144 us
  local copies, waits for them, and re-layouts: 32.3 us -> 13.1 us
  starting transfers between devices: 1.11 us -> 3.98 us
    pallas_call x1, Pallas kernels: 168 us -> 144 us  [exchange(): pl.pallas_call(functools.partial(exchange_kernel, nz, ny, rank, shards, m...]
    reshape x6 -> x0, local copies, waits for them, and re-layouts: 13.1 us -> none  [the longest x4 9.78 us: grouped(): rows.reshape(-1, shards, ny, part).transpose(2, 0, 1, 3)]
    another operation x3 -> x0, local copies, waits for them, and re-layouts: 3.99 us -> none  [the longest x1 2.8 us: local(): down_grad.reshape(owned, rank, width)]
    transpose x2 -> x1, local copies, waits for them, and re-layouts: 3.65 us -> 0.15 us  [joined(): groups.reshape(ny, -1, shards, part).transpose(1, 2, 0, 3)]
    unnamed x25 -> x21, local copies, waits for them, and re-layouts: 5.35 us -> 7 us
  transfers between devices with their start and end apart: 3 -> 3, of which waited for: 1 -> 1; matrix products, arithmetic and copies ran while one was open for 15% -> 8% of each run, Pallas kernels for 67% -> 70%
where the time goes in v2:
time: 207 us
  Pallas kernels  144 us (70%)
  matrix products  20.6 us (10%)
  between operations  14.3 us (7%)
  local copies, waits for them, and re-layouts  13.1 us (6%)
  waiting for transfers between devices  11.3 us (5%)
  starting transfers between devices  3.98 us (2%)
    pallas_call x1, Pallas kernels, exchange(): pl.pallas_call(functools.partial(exchange_kernel, nz, ny, rank, shards, m...  144 us
    ppermute x1, waiting for transfers between devices, local(): got = lax.ppermute(grads_of(to), 'adapter', pairs[d])  11.2 us
    unnamed x21, local copies, waits for them, and re-layouts  7 us
    dot_general x2, matrix products, grads_of(): lax.dot_general(og, weight, (((1,), (1,)), ((), ())), preferred_element_t...  6.67 us
    dot_general x2, matrix products, base_of(): return jnp.dot(x, weight, preferred_element_type=jnp.float32)  6.36 us
    dot_general x2, matrix products, grads_of(): lax.dot_general(lg, a_flat, (((0,), (0,)), ((), ())), preferred_element_t...  5.23 us
  transfers between devices with their start and end apart: 3, of which 1 were waited for; matrix products, arithmetic and copies ran while one was open for 8% of the time, Pallas kernels for 70%

profile of v2, /device:TPU:14, one launch (start us, length us, event | category | flops | bytes accessed | tf_op | source)
XLA Modules:
  0.0 207.0 jit_solution(15701957195541964308)
XLA Ops:
  7.2 0.0 all-gather.2.cloned.1.call-start
  7.2 3.1 %constant_dynamic-slice_fusion = bf16[1024,1024]{1,0:T(8,128)(2,1)} fusion(bf16[2048,1024]{1,0:T(8,128)(2,1)} %param.8, s32[]{:T(128)S(6)} %select_n.22), kind=kLoop, calls=%fused_computation.30 | loop fusion | bytes 4194308 | tf_op jit(solution)/shard_map/dynamic_slice | solution.py:455
  10.3 0.0 all-gather.2.cloned.1.call-update
  10.3 143.9 %shard_map.93 = (bf16[8,64,4096]{2,1,0:T(8,128)(2,1)}, bf16[8,64,1024]{2,1,0:T(8,128)(2,1)}, bf16[256,4096]{1,0:T(8,128)(2,1)}, bf16[256,1024]{1,0:T(8,128)(2,1)...) custom-call(s32[1,128]{1,0:T(1,128)} %bitcast.37, ...), custom_call_target="tpu_custom_call" | custom-call | tf_op jit(solution)/shard_map/pallas_call | solution.py:395
  154.3 0.0 copy-start
  154.3 0.0 copy-start.4
  154.3 4.5 %fusion.3 = f32[128,4096]{1,0:T(8,128)} fusion(bf16[512,4096]{1,0:T(8,128)(2,1)} %bitcast.25, bf16[512,256]{1,0:T(8,128)(2,1)} %bitcast.32, s32[]{:T(128)S(6)} %select_n.23), kind=kOutput, calls=%fused_computation.7 | convolution fusion | flops 537919488 | bytes 6422532 | tf_op jit(solution)/shard_map/dot_general | solution.py:478
  158.8 0.0 copy-done
  158.8 0.0 copy-done.4
  158.8 0.8 fusion.2
  159.5 0.0 all-gather.2.cloned.1.call-done
  159.6 0.0 slice-start
  159.6 0.0 slice-start.1
  159.6 0.0 copy-start.1
  159.6 0.0 copy-start.3
  159.6 5.1 %convolution_convert_fusion.2 = bf16[128,1024]{1,0:T(8,128)(2,1)S(1)} fusion(bf16[4096,1024]{1,0:T(8,128)(2,1)} %all-gather.2.cloned.1.call-done, bf16[256,4096]{1,0:T(8,128)(2,1)} %get-tuple-element.12, s32[]{:T(128)S(6)} %select_n.23), kind=kOutput, calls=%fused_computation.12 | convolution fusion | flops 1073872896 | bytes 9699332 | tf_op jit(solution)/shard_map/dot_general | solution.py:488
  164.7 2.4 %collective-permute-start = (bf16[128,1024]{1,0:T(8,128)(2,1)S(1)}, bf16[128,1024]{1,0:T(8,128)(2,1)}, u32[]{:S(2)}, u32[]{:S(2)}) collective-permute-start(bf16[128,1024]{1,0:T(8,128)(2,1)S(1)} %convolution_convert_fusion.2), channel_id=1, source_target_pairs={{0,1},{1,0},{2,3},{3,2},{4,5},{5,4},{6,7},{7,6},{8,9},{9,8},{10,11... | collective-permute-start | bytes 786440 | tf_op jit(solution)/shard_map/ppermute | solution.py:496
  167.1 0.0 slice-done
  167.1 0.0 slice-done.1
  167.1 0.0 copy-done.1
  167.1 0.0 copy-done.3
  167.1 3.8 %fusion = bf16[128,4096]{1,0:T(8,128)(2,1)} fusion(f32[128,4096]{1,0:T(8,128)S(1)} %copy-done.1, bf16[4096,1024]{1,0:T(8,128)(2,1)S(1)} %bitcast.24, bf16[256,1024]{1,0:T(8,128)(2,1)S(1)} %copy-done.3, s32[]{:T(128)S(6)} %select_n.23), kind=kOutput, calls=%fused_computation.2 | convolution fusion | flops 1074790400 | bytes 11796484 | tf_op jit(solution)/shard_map/dot_general | solution.py:481
  171.0 0.0 copy-start.2
  171.0 1.5 collective-permute-start.1
  172.5 2.8 %fusion.4 = bf16[1,128,4096]{2,1,0:T(8,128)(2,1)S(1)} fusion(f32[128,4096]{1,0:T(8,128)S(1)} %fusion.2, bf16[4096,1024]{1,0:T(8,128)(2,1)S(1)} %bitcast.24, bf16[256,1024]{1,0:T(8,128)(2,1)S(1)} %copy-done.3, s32[]{:T(128)S(6)} %select_n.21), kind=kOutput, calls=%fused_computation.8 | convolution fusion | flops 1074790400 | bytes 11796484 | tf_op jit(solution)/shard_map/dot_general | solution.py:481
  175.4 0.0 copy-done.2
  175.4 1.3 fusion.8
  176.6 0.0 copy-start.6
  176.6 0.7 copy.13
  177.3 0.0 collective-permute-done
  177.3 0.3 copy-done.6
  177.6 2.3 %add_convert_fusion = bf16[128,1024]{1,0:T(8,128)(2,1)} fusion(f32[128,1024]{1,0:T(8,128)S(1)} %fusion.8, bf16[128,1024]{1,0:T(8,128)(2,1)} %collective-permute-done, bf16[512,1024]{1,0:T(8,128)(2,1)} %bitcast.30, bf16[512,256]{1,0:T(8,128)(2,1)S(1)} %bitcast.36, s32[]{:T(128)S(6)} %select_n.21), kind=kOutput, calls=%fused_computation.16 | convolution fusion | flops 135135232 | bytes 2228228 | tf_op jit(solution)/shard_map/dot_general | solution.py:506
  179.9 11.2 %collective-permute-done.1 = bf16[128,4096]{1,0:T(8,128)(2,1)} collective-permute-done((bf16[128,4096]{1,0:T(8,128)(2,1)}, bf16[128,4096]{1,0:T(8,128)(2,1)}, u32[]{:S(2)}, u32[]{:S(2)}) %collective-permute-start.1) | collective-permute-done | bytes 1048608 | tf_op jit(solution)/shard_map/ppermute | solution.py:494
  191.1 1.6 copy.12
  192.7 0.3 broadcast_in_dim.10
  193.0 0.1 constant_dynamic-update-slice_fusion.1
  193.2 0.1 constant_dynamic-update-slice_fusion
  193.3 0.1 copy.14
  193.5 2.9 %copy.15 = bf16[128,8192]{1,0:T(8,128)(2,1)} copy(bf16[128,8192]{0,1:T(8,128)(2,1)S(1)} %bitcast.28) | data formatting | bytes 4194304
  196.4 0.0 copy-start.5
  196.4 3.1 %copy.20 = f32[4,16,8192]{2,1,0:T(8,128)} copy(f32[4,16,8192]{2,1,0:T(8,128)} %bitcast.29) | data formatting | bytes 4194304
  199.5 0.0 copy-done.5
  199.5 0.7 copy.21
  (1 shorter events, 0.0 us)
Async XLA Ops:
  7.2 152.4 %all-gather.2.cloned.1.call-start = ((), (), s32[]{:S(2)}) async-start(), calls=%async_computation | async-start | bytes 10485760 | tf_op jit(solution)/shard_map/all_gather | solution.py:456
  154.3 4.5 %copy-start = (bf16[8,64,4096]{2,1,0:T(8,128)(2,1)S(1)}, bf16[8,64,4096]{2,1,0:T(8,128)(2,1)}, u32[]{:S(2)}) copy-start(bf16[8,64,4096]{2,1,0:T(8,128)(2,1)} %get-tuple-element.17) | copy-start | bytes 12582916
  154.3 4.5 %copy-start.4 = (bf16[8,64,256]{2,1,0:T(8,128)(2,1)S(1)}, bf16[8,64,256]{2,1,0:T(8,128)(2,1)}, u32[]{:S(2)}) copy-start(bf16[8,64,256]{2,1,0:T(8,128)(2,1)} %get-tuple-element.16) | copy-start | bytes 786436
  159.6 7.6 %slice-start = ((s8[8388608]{0:T(1024)(128)(4,1)}), s8[4194304]{0:T(1024)(128)(4,1)S(1)}, s32[]{:S(2)}) async-start(s8[8388608]{0:T(1024)(128)(4,1)} %bitcast.23), calls=%async_computation.1 | async-start | bytes 8388608
  159.6 7.5 %slice-start.1 = ((s8[8388608]{0:T(1024)(128)(4,1)}), s8[4194304]{0:T(1024)(128)(4,1)S(1)}, s32[]{:S(2)}) async-start(s8[8388608]{0:T(1024)(128)(4,1)} %bitcast.23), calls=%async_computation.2 | async-start | bytes 8388608
  159.6 7.5 %copy-start.1 = (f32[128,4096]{1,0:T(8,128)S(1)}, f32[128,4096]{1,0:T(8,128)}, u32[]{:S(2)}) copy-start(f32[128,4096]{1,0:T(8,128)} %fusion.3) | copy-start | bytes 6291460
  159.6 7.5 %copy-start.3 = (bf16[256,1024]{1,0:T(8,128)(2,1)S(1)}, bf16[256,1024]{1,0:T(8,128)(2,1)}, u32[]{:S(2)}) copy-start(bf16[256,1024]{1,0:T(8,128)(2,1)} %get-tuple-element.15) | copy-start | bytes 1572868
  164.7 12.6 %collective-permute-start = (bf16[128,1024]{1,0:T(8,128)(2,1)S(1)}, bf16[128,1024]{1,0:T(8,128)(2,1)}, u32[]{:S(2)}, u32[]{:S(2)}) collective-permute-start(bf16[128,1024]{1,0:T(8,128)(2,1)S(1)} %convolution_convert_fusion.2), channel_id=1, source_target_pairs={{0,1},{1,0},{2,3},{3,2},{4,5},{5,4},{6,7},{7,6},{8,9},{9,8},{10,11... | collective-permute-start | bytes 786440 | tf_op jit(solution)/shard_map/ppermute | solution.py:496
  171.0 4.4 %copy-start.2 = (bf16[256,4096]{1,0:T(8,128)(2,1)S(1)}, bf16[256,4096]{1,0:T(8,128)(2,1)}, u32[]{:S(2)}) copy-start(bf16[256,4096]{1,0:T(8,128)(2,1)} %get-tuple-element.12) | copy-start | bytes 6291460
  171.0 20.2 %collective-permute-start.1 = (bf16[128,4096]{1,0:T(8,128)(2,1)}, bf16[128,4096]{1,0:T(8,128)(2,1)}, u32[]{:S(2)}, u32[]{:S(2)}) collective-permute-start(bf16[128,4096]{1,0:T(8,128)(2,1)} %fusion), channel_id=1, source_target_pairs={{0,1},{1,0},{2,3},{3,2},{4,5},{5,4},{6,7},{7,6},{8,9},{9,8},{10,11... | collective-permute-start | bytes 3145736 | tf_op jit(solution)/shard_map/ppermute | solution.py:494
  176.6 1.0 copy-start.6
  196.4 3.1 %copy-start.5 = (f32[64,1024]{1,0:T(8,128)S(1)}, f32[64,1024]{1,0:T(8,128)}, u32[]{:S(2)}) copy-start(f32[64,1024]{1,0:T(8,128)} %get-tuple-element.19) | copy-start | bytes 786436
Sparse Core Ops, SparseCore 0:
  10.4 58.4 all-gather.1

commit v3 on v2

--- a/solution.py
+++ b/solution.py
@@ -19,10 +19,10 @@
 
 
 def exchange_kernel(
-    nz, ny, rank, shards, tile,
+    nz, ny, rank, tile,
     idx_ref, a_ref, b_ref, x_ref, og_ref,
-    a_all, b_all, x_all, og_all, lg_t, low_all, dg_full, up_full,
-    gbuf, rin, rin2, ubuf, uin, uin2, low_part, low_in, dg_out, dg_in, up_out, up_in,
+    b_all, low_all, side_full, dg_full, up_full,
+    a_all, x_all, og_all, lg_t, side_out, gbuf, rin, rin2, ubuf, uin, uin2, low_part, low_in, dg_out, dg_in, up_out, up_in,
     loc_sem, ag_send, ag_recv, b_send, b_recv, y_send, y_recv,
     rs_send, rs_recv, rs_recv2, us_send, us_recv, us_recv2,
 ):
@@ -31,7 +31,6 @@
     y = lax.rem(me, ny)
     rows, width = a_all.shape[1:]
     tok = og_ref.shape[0]
-    part = width // shards
     vcols = ubuf.shape[2]
     owned = rows // rank
     nb = nz * ny
@@ -76,16 +75,11 @@
         c.start()
         sends.append(c)
 
-    def pieces(src, j, dst):
-        for q in range(shards):
-            at = pl.ds(pl.multiple_of((q * ny + j) * part, part), part)
-            yield src.at[:, at], dst.at[:, pl.ds(q * part, part)]
+    def group(j):
+        return pl.ds(pl.multiple_of(j * width, width), width)
 
     def y_start_columns(kind, d, src, dst):
-        ssem, rsem, dev = y_send.at[kind, d - 1], y_recv.at[kind, d - 1], z * ny + peer(d)
-        for piece, to in pieces(src, peer(d), dst):
-            copy_to(piece, to, ssem, rsem, dev).start()
-        sends.append(copy_to(dst, dst, ssem, rsem, dev))
+        y_start(kind, d, src.at[:, group(peer(d))], dst)
 
     def y_wait(kind, d, dst):
         copy_to(
@@ -99,10 +93,10 @@
     keep_b = pltpu.make_async_copy(b_ref, b_all.at[me], loc_sem.at[0])
     keep_og = pltpu.make_async_copy(og_ref, og_all.at[slot(y)], loc_sem.at[3])
     keep_b.start()
-    for src, dst in pieces(a_ref, y, a_all.at[me]):
-        pltpu.make_async_copy(src, dst, loc_sem.at[1]).start()
-    for src, dst in pieces(x_ref, y, x_all.at[slot(y)]):
-        pltpu.make_async_copy(src, dst, loc_sem.at[2]).start()
+    keep_a = pltpu.make_async_copy(a_ref.at[:, group(y)], a_all.at[me], loc_sem.at[1])
+    keep_x = pltpu.make_async_copy(x_ref.at[:, group(y)], x_all.at[slot(y)], loc_sem.at[2])
+    keep_a.start()
+    keep_x.start()
     keep_og.start()
 
     def hop(buf, ssem, rsem, s, ys, last=False):
@@ -156,7 +150,7 @@
 
     keep_b.wait()
     hop_b(0)
-    pltpu.make_async_copy(a_all.at[me], a_all.at[me], loc_sem.at[1]).wait()
+    keep_a.wait()
     hop_own(0)
     hop_b(1)
     for s in range(2, nz):
@@ -183,7 +177,7 @@
     keep_og.wait()
     for d in range(1, ny):
         y_start(3, d, og_ref, og_all.at[slot(y)])
-    pltpu.make_async_copy(x_all.at[slot(y)], x_all.at[slot(y)], loc_sem.at[2]).wait()
+    keep_x.wait()
     for d in range(1, ny):
         y_wait(1, d, x_all.at[slot(back(d))])
         y_wait(4, d, lg_t.at[:, :, slot(back(d))])
@@ -287,9 +281,7 @@
             yield d
 
     def down_at(j, start, values):
-        q = start // part
-        at = pl.multiple_of((q * ny + j) * part + start - q * part, tile)
-        dg_full[:, pl.ds(at, tile)] = values
+        dg_full[:, pl.ds(pl.multiple_of(j * width + start, tile), tile)] = values
 
     def up_at(j, start, values):
         up_full[:, pl.ds(pl.multiple_of(j * vcols, vcols), vcols)] = adapter_scale * values
@@ -317,8 +309,24 @@
                 preferred_element_type=jnp.float32,
             )
 
+    def side_rows(j, put):
+        @pl.loop(0, width // tile)
+        def _(i):
+            start = pl.multiple_of(i * tile, tile)
+            cols = pl.ds(start, tile)
+            acc = lax.dot_general(
+                lg_t[:, :, slot(j)].reshape(nb * rows, tok), a_all[:, :, cols].reshape(nb * rows, tile),
+                (((0,), (0,)), ((), ())), preferred_element_type=jnp.float32,
+            )
+            put(start, cols, acc.astype(jnp.bfloat16))
+
     for d in range(1, ny):
         y_start(5, d, low_part.at[peer(d)], low_in.at[d - 1])
+    for d in range(1, ny):
+        def put_peer(start, cols, values):
+            side_out[d - 1, :, cols] = values
+
+        side_rows(peer(d), put_peer)
     for d in range(1, ny):
         y_wait(5, d, low_in.at[d - 1])
 
@@ -334,11 +342,18 @@
     for d in range(1, ny):
         y_start(6, d, low_all.at[:, :, slot(y)], low_all.at[:, :, slot(y)])
     for d in range(1, ny):
+        y_start(9, d, side_out.at[d - 1], side_full.at[:, group(y)])
+    for d in range(1, ny):
         y_wait(3, d, og_all.at[slot(back(d))])
         y_wait(6, d, low_all.at[:, :, slot(back(d))])
 
     for t in range(nz - 1):
         reduce_step(t, *up)
+
+    def put_own(start, cols, values):
+        side_full[:, pl.ds(pl.multiple_of(y * width + start, tile), tile)] = values
+
+    side_rows(y, put_own)
     for d in reduce_end(
         lg_t, x_acts, down_at, dg_out, rin, rin2, rs_recv, rs_recv2, width, tile
     ):
@@ -360,6 +375,8 @@
             start = pl.multiple_of(i * tile, tile)
             down_at(back(d), start, dg_in[d - 1, :, pl.ds(start, tile)].astype(jnp.float32))
 
+    for d in range(1, ny):
+        y_wait(9, d, side_full.at[:, group(back(d))])
     for c in sends:
         c.wait_send()
     for s in range(nz):
@@ -371,7 +388,7 @@
         reduce_step(t, *up, last=True)
 
 
-def exchange(nz, ny, shards, rank, idx, a_rows, b_rows, tokens, grads):
+def exchange(nz, ny, rank, idx, a_rows, b_rows, tokens, grads):
     nb = nz * ny
     rows = a_rows.shape[0]
     width = a_rows.shape[1] // ny
@@ -381,25 +398,25 @@
     bf, f32 = jnp.bfloat16, jnp.float32
     peers = max(1, ny - 1)
     outs = [
-        ((nb, rows, width), bf),
         ((nb, rows, kv_width), bf),
-        ((ny * tok_rows, width), bf),
-        ((ny * tok_rows, kv_width), bf),
         ((nb, rows, ny * tok_rows), bf),
-        ((nb, rows, ny * tok_rows), bf),
+        ((tok_rows, ny * width), bf),
         ((rows, ny * width), f32),
         ((rows, kv_width), f32),
     ]
     vmem = pl.BlockSpec(memory_space=pltpu.VMEM)
     dma = pltpu.SemaphoreType.DMA
     return pl.pallas_call(
-        functools.partial(
-            exchange_kernel, nz, ny, rank, shards, min(512, width // shards)
-        ),
+        functools.partial(exchange_kernel, nz, ny, rank, min(512, width)),
         out_shape=[jax.ShapeDtypeStruct(s, t) for s, t in outs],
         in_specs=[vmem] * 5,
         out_specs=[vmem] * len(outs),
         scratch_shapes=[
+            pltpu.VMEM((nb, rows, width), bf),
+            pltpu.VMEM((ny * tok_rows, width), bf),
+            pltpu.VMEM((ny * tok_rows, kv_width), bf),
+            pltpu.VMEM((nb, rows, ny * tok_rows), bf),
+            pltpu.VMEM((peers, tok_rows, width), bf),
             pltpu.VMEM((nb, rows, width), bf),
             pltpu.VMEM((nb, rows, width), bf),
             pltpu.VMEM((ny, rows, width), bf),
@@ -417,8 +434,8 @@
             dma((nb,)),
             dma((2, nb)),
             dma((nb,)),
-            dma((9, peers)),
-            dma((9, peers)),
+            dma((10, peers)),
+            dma((10, peers)),
             dma((nz,)),
             dma((nz,)),
             dma((1,)),
@@ -441,22 +458,14 @@
     output_gradient,
 ):
     owners = lax.axis_size("adapter")
-    shards = lax.axis_size("dp")
     nz, ny = grid_sides(owners)
     owned, rank, width = adapter_down_factors.shape
     tok_rows = tokens.shape[0]
     kv_width = output_gradient.shape[1]
-    part = frozen_value_weight.shape[0] // ny
     y = lax.rem(lax.axis_index("adapter"), ny)
-
-    def joined(groups):
-        return groups.reshape(ny, -1, shards, part).transpose(1, 2, 0, 3).reshape(-1, width)
-
-    own_weight = lax.dynamic_slice_in_dim(frozen_value_weight, y * part, part, 0)
-    weight = lax.all_gather(own_weight, "dp", axis=0, tiled=True)
-
-    a_all, b_all, x_all, og_all, lg_t, low_all, down_grad, up_factor_gradient = exchange(
-        nz, ny, shards, rank,
+    weight = lax.all_gather(frozen_value_weight, "dp", axis=0, tiled=True)
+    b_all, low_all, side, down_grad, up_factor_gradient = exchange(
+        nz, ny, rank,
         token_adapter_index.reshape(1, tok_rows),
         adapter_down_factors.reshape(owned * rank, width),
         adapter_up_factors.reshape(owned * rank, kv_width),
@@ -464,40 +473,6 @@
         output_gradient,
     )
     slots = owners * owned * rank
-    a_flat = a_all.reshape(slots, shards * part)
-    pairs = {
-        d: [(z * ny + i, z * ny + (i + d) % ny) for z in range(nz) for i in range(ny)]
-        for d in range(1, ny)
-    }
-
-    def grads_of(j):
-        lg = lax.dynamic_slice_in_dim(
-            lg_t.reshape(slots, ny * tok_rows), j * tok_rows, tok_rows, 1
-        )
-        og = lax.dynamic_slice_in_dim(og_all, j * tok_rows, tok_rows, 0)
-        side = lax.dot_general(
-            lg, a_flat, (((0,), (0,)), ((), ())), preferred_element_type=jnp.float32
-        ).astype(jnp.bfloat16)
-        back = lax.dot_general(
-            og, weight, (((1,), (1,)), ((), ())), preferred_element_type=jnp.float32
-        )
-        return (back + side).astype(jnp.bfloat16)
-
-    def base_of(j):
-        x = lax.dynamic_slice_in_dim(x_all, j * tok_rows, tok_rows, 0)
-        return jnp.dot(x, weight, preferred_element_type=jnp.float32)
-
-    grad_parts = jnp.zeros((ny, tok_rows, shards * part), jnp.bfloat16)
-    base = base_of(y)
-    for d in range(1, ny):
-        to = lax.rem(y + d, ny)
-        got = lax.ppermute(grads_of(to), "adapter", pairs[d])
-        grad_parts = lax.dynamic_update_index_in_dim(grad_parts, got, lax.rem(y + ny - d, ny), 0)
-        base += lax.ppermute(base_of(to).astype(jnp.bfloat16), "adapter", pairs[d]).astype(
-            jnp.float32
-        )
-    grad_parts = lax.dynamic_update_index_in_dim(grad_parts, grads_of(y), y, 0)
-    token_grad = joined(grad_parts)
     low_own = lax.dynamic_slice_in_dim(
         low_all.reshape(slots, ny * tok_rows), y * tok_rows, tok_rows, 1
     )
@@ -508,11 +483,13 @@
             preferred_element_type=jnp.float32,
         )
     ).astype(jnp.bfloat16)
-    result = (base + lifted).astype(jnp.bfloat16)
-
+    base = jnp.dot(tokens, weight, preferred_element_type=jnp.float32)
+    back = lax.dot_general(
+        output_gradient, weight, (((1,), (1,)), ((), ())), preferred_element_type=jnp.float32
+    )
     return (
-        result,
-        token_grad,
+        (base + lifted).astype(jnp.bfloat16),
+        (back + side).astype(jnp.bfloat16),
         down_grad.reshape(owned, rank, width),
         up_factor_gradient.reshape(owned, rank, kv_width),
     )

time: 207 us -> 194 us (0.937)
  local copies, waits for them, and re-layouts: 13.1 us -> 2.04 us
  waiting for transfers between devices: 11.3 us -> 0.7 us
  Pallas kernels: 144 us -> 153 us
  starting transfers between devices: 3.98 us -> 0.04 us
  matrix products: 20.6 us -> 24 us
    ppermute x2 -> x0, waiting for transfers between devices: 11.2 us -> none  [the longest x1 11.2 us: local(): got = lax.ppermute(grads_of(to), 'adapter', pairs[d])]
    pallas_call x1, Pallas kernels: 144 us -> 153 us  [exchange(): pl.pallas_call(functools.partial(exchange_kernel, nz, ny, rank, min(512,...]
    unnamed x21 -> x10, local copies, waits for them, and re-layouts: 7 us -> 2.04 us
    dot_general x6 -> x2, matrix products: 18.3 us -> 22.3 us  [the longest x1 13.5 us: local(): lax.dot_general(output_gradient, weight, (((1,), (1,)), ((), ())), prefer...]
    ppermute x2 -> x0, starting transfers between devices: 3.94 us -> none  [the longest x1 2.4 us: local(): lax.ppermute(base_of(to).astype(jnp.bfloat16), 'adapter', pairs[d])]
    dynamic_slice x1 -> x0, local copies, waits for them, and re-layouts: 3.08 us -> none  [local(): lax.dynamic_slice_in_dim(frozen_value_weight, y * part, part, 0)]
    broadcast_in_dim x3 -> x0, local copies, waits for them, and re-layouts: 2.55 us -> none  [the longest x1 1.61 us: local(): lax.dynamic_update_index_in_dim(grad_parts, got, lax.rem(y + ny - d, ny), 0)]
  transfers between devices with their start and end apart: 3 -> 1, of which waited for: 1 -> 0; matrix products, arithmetic and copies ran while one was open for 8% -> 1% of each run, Pallas kernels for 70% -> 79%
where the time goes in v3:
time: 194 us; the launch traced here: 193 us
  Pallas kernels  153 us (79%)
  matrix products  24 us (12%)
  between operations  14.1 us (7%)
  local copies, waits for them, and re-layouts  2.04 us (1%)
    pallas_call x1, Pallas kernels, exchange(): pl.pallas_call(functools.partial(exchange_kernel, nz, ny, rank, min(512,...  153 us
    dot_general x1, matrix products, local(): lax.dot_general(output_gradient, weight, (((1,), (1,)), ((), ())), prefer...  13.5 us
    dot_general x1, matrix products, local(): base = jnp.dot(tokens, weight, preferred_element_type=jnp.float32)  8.84 us
  transfers between devices with their start and end apart: 1, of which 0 were waited for; matrix products, arithmetic and copies ran while one was open for 1% of the time, Pallas kernels for 79%

profile of v3, /device:TPU:14, one launch (start us, length us, event | category | flops | bytes accessed | tf_op | source)
XLA Modules:
  0.0 193.5 jit_solution(9411763483315815887)
XLA Ops:
  7.2 0.0 copy-start
  7.2 0.0 all-gather.2.cloned.1.call-start
  7.2 0.7 all-gather.2.cloned.1.call-update
  7.9 152.6 %shard_map.93 = (bf16[8,64,1024]{2,1,0:T(8,128)(2,1)}, bf16[8,64,256]{2,1,0:T(8,128)(2,1)}, bf16[128,8192]{1,0:T(8,128)(2,1)}, f32[64,8192]{1,0:T(8,128)}, f32[64,1024]{1,0:T(8,128)}) custom-call(s32[1,128]{1,0:T(1,128)} %bitcast.18, bf16[64,8192]{1,0:T(8,128)(2,1)} %bitcast.14, bf16[64,1024]{1,0:T(8,128)(2,1)} %bitcast.16, bf16[128,8192]{1,0:T(8,128)(2,1)} %x_ref.1, ...), custom_call_target="tpu_custom_call" | custom-call | tf_op jit(solution)/shard_map/pallas_call | solution.py:409
  160.5 1.6 fusion.2
  162.2 0.0 copy-start.2
  162.2 0.0 all-gather.2.cloned.1.call-done
  162.2 0.0 copy-done
  162.2 8.8 %fusion.3 = bf16[128,1024]{1,0:T(8,128)(2,1)} fusion(f32[128,1024]{1,0:T(8,128)S(1)} %fusion.2, bf16[128,8192]{1,0:T(8,128)(2,1)S(1)} %copy-done, bf16[8192,1024]{1,0:T(8,128)(2,1)} %all-gather.2.cloned.1.call-done), kind=kOutput, calls=%fused_computation.6 | convolution fusion | flops 2147745792 | bytes 19660800 | tf_op jit(solution)/shard_map/dot_general | solution.py:486
  171.1 0.0 copy-done.2
  171.1 0.0 copy-start.1
  171.1 13.5 %fusion = bf16[128,8192]{1,0:T(8,128)(2,1)} fusion(bf16[128,1024]{1,0:T(8,128)(2,1)S(1)} %copy-done.2, bf16[8192,1024]{1,0:T(8,128)(2,1)} %all-gather.2.cloned.1.call-done, bf16[128,8192]{1,0:T(8,128)(2,1)} %get-tuple-element.11), kind=kOutput, calls=%fused_computation.1 | convolution fusion | flops 2150629376 | bytes 21233664 | tf_op jit(solution)/shard_map/dot_general | solution.py:487
  184.6 0.0 copy-done.1
  184.6 0.0 copy-start.3
  184.6 1.3 copy.12
  185.9 0.0 copy-done.3
  185.9 0.7 copy.13
Async XLA Ops:
  7.2 155.1 %copy-start = (bf16[128,8192]{1,0:T(8,128)(2,1)S(1)}, bf16[128,8192]{1,0:T(8,128)(2,1)}, u32[]{:S(2)}) copy-start(bf16[128,8192]{1,0:T(8,128)(2,1)} %x_ref.1) | copy-start | bytes 6291460
  7.2 155.1 %all-gather.2.cloned.1.call-start = ((), (), s32[]{:S(2)}) async-start(), calls=%async_computation | async-start | bytes 20971520 | tf_op jit(solution)/shard_map/all_gather | solution.py:466
  162.2 8.9 %copy-start.2 = (bf16[128,1024]{1,0:T(8,128)(2,1)S(1)}, bf16[128,1024]{1,0:T(8,128)(2,1)}, u32[]{:S(2)}) copy-start(bf16[128,1024]{1,0:T(8,128)(2,1)} %og_ref.1) | copy-start | bytes 786436
  171.1 13.5 %copy-start.1 = (f32[64,8192]{1,0:T(8,128)S(1)}, f32[64,8192]{1,0:T(8,128)}, u32[]{:S(2)}) copy-start(f32[64,8192]{1,0:T(8,128)} %get-tuple-element.12) | copy-start | bytes 6291460
  184.6 1.3 copy-start.3
Sparse Core Ops, SparseCore 0:
  9.6 106.0 all-gather.1

commit v4 on v3

--- a/solution.py
+++ b/solution.py
@@ -152,6 +152,8 @@
     hop_b(0)
     keep_a.wait()
     hop_own(0)
+    for d in range(1, ny):
+        y_start_columns(2, d, a_ref, a_all.at[me])
     hop_b(1)
     for s in range(2, nz):
         hop_b(s)
@@ -172,8 +174,6 @@
     lax.fori_loop(0, nb, lg_block, 0)
     for d in range(1, ny):
         y_start(4, d, lg_t.at[:, :, slot(y)], lg_t.at[:, :, slot(y)])
-    for d in range(1, ny):
-        y_start_columns(2, d, a_ref, a_all.at[me])
     keep_og.wait()
     for d in range(1, ny):
         y_start(3, d, og_ref, og_all.at[slot(y)])

time: 194 us -> 207 us (1.067)
  Pallas kernels: 153 us -> 165 us
    pallas_call x1, Pallas kernels: 153 us -> 165 us  [exchange(): pl.pallas_call(functools.partial(exchange_kernel, nz, ny, rank, min(512,...]
  transfers between devices with their start and end apart: 1 -> 1, of which waited for: 0 -> 0; matrix products, arithmetic and copies ran while one was open for 1% -> 1% of each run, Pallas kernels for 79% -> 80%
where the time goes in v4:
time: 207 us; the launch traced here: 206 us
  Pallas kernels  165 us (80%)
  matrix products  23.9 us (12%)
  between operations  14.1 us (7%)
    pallas_call x1, Pallas kernels, exchange(): pl.pallas_call(functools.partial(exchange_kernel, nz, ny, rank, min(512,...  165 us
    dot_general x1, matrix products, local(): lax.dot_general(output_gradient, weight, (((1,), (1,)), ((), ())), prefer...  13.5 us
    dot_general x1, matrix products, local(): base = jnp.dot(tokens, weight, preferred_element_type=jnp.float32)  8.84 us
  transfers between devices with their start and end apart: 1, of which 0 were waited for; matrix products, arithmetic and copies ran while one was open for 1% of the time, Pallas kernels for 80%

profile of v4, /device:TPU:14, one launch (start us, length us, event | category | flops | bytes accessed | tf_op | source)
XLA Modules:
  0.0 206.0 jit_solution(6560671851661671066)
XLA Ops:
  7.2 0.0 copy-start
  7.2 0.0 all-gather.2.cloned.1.call-start
  7.2 0.7 all-gather.2.cloned.1.call-update
  7.9 165.2 %shard_map.93 = (bf16[8,64,1024]{2,1,0:T(8,128)(2,1)}, bf16[8,64,256]{2,1,0:T(8,128)(2,1)}, bf16[128,8192]{1,0:T(8,128)(2,1)}, f32[64,8192]{1,0:T(8,128)}, f32[64,1024]{1,0:T(8,128)}) custom-call(s32[1,128]{1,0:T(1,128)} %bitcast.18, bf16[64,8192]{1,0:T(8,128)(2,1)} %bitcast.14, bf16[64,1024]{1,0:T(8,128)(2,1)} %bitcast.16, bf16[128,8192]{1,0:T(8,128)(2,1)} %x_ref.1, ...), custom_call_target="tpu_custom_call" | custom-call | tf_op jit(solution)/shard_map/pallas_call | solution.py:409
  173.2 1.6 fusion.2
  174.8 0.0 copy-start.2
  174.8 0.0 all-gather.2.cloned.1.call-done
  174.8 0.0 copy-done
  174.9 8.8 %fusion.3 = bf16[128,1024]{1,0:T(8,128)(2,1)} fusion(f32[128,1024]{1,0:T(8,128)S(1)} %fusion.2, bf16[128,8192]{1,0:T(8,128)(2,1)S(1)} %copy-done, bf16[8192,1024]{1,0:T(8,128)(2,1)} %all-gather.2.cloned.1.call-done), kind=kOutput, calls=%fused_computation.6 | convolution fusion | flops 2147745792 | bytes 19660800 | tf_op jit(solution)/shard_map/dot_general | solution.py:486
  183.7 0.0 copy-done.2
  183.7 0.0 copy-start.1
  183.7 13.5 %fusion = bf16[128,8192]{1,0:T(8,128)(2,1)} fusion(bf16[128,1024]{1,0:T(8,128)(2,1)S(1)} %copy-done.2, bf16[8192,1024]{1,0:T(8,128)(2,1)} %all-gather.2.cloned.1.call-done, bf16[128,8192]{1,0:T(8,128)(2,1)} %get-tuple-element.11), kind=kOutput, calls=%fused_computation.1 | convolution fusion | flops 2150629376 | bytes 21233664 | tf_op jit(solution)/shard_map/dot_general | solution.py:487
  197.2 0.0 copy-done.1
  197.2 0.0 copy-start.3
  197.2 1.3 copy.12
  198.5 0.0 copy-done.3
  198.5 0.7 copy.13
Async XLA Ops:
  7.2 167.7 %copy-start = (bf16[128,8192]{1,0:T(8,128)(2,1)S(1)}, bf16[128,8192]{1,0:T(8,128)(2,1)}, u32[]{:S(2)}) copy-start(bf16[128,8192]{1,0:T(8,128)(2,1)} %x_ref.1) | copy-start | bytes 6291460
  7.2 167.7 %all-gather.2.cloned.1.call-start = ((), (), s32[]{:S(2)}) async-start(), calls=%async_computation | async-start | bytes 20971520 | tf_op jit(solution)/shard_map/all_gather | solution.py:466
  174.8 8.9 %copy-start.2 = (bf16[128,1024]{1,0:T(8,128)(2,1)S(1)}, bf16[128,1024]{1,0:T(8,128)(2,1)}, u32[]{:S(2)}) copy-start(bf16[128,1024]{1,0:T(8,128)(2,1)} %og_ref.1) | copy-start | bytes 786436
  183.7 13.5 %copy-start.1 = (f32[64,8192]{1,0:T(8,128)S(1)}, f32[64,8192]{1,0:T(8,128)}, u32[]{:S(2)}) copy-start(f32[64,8192]{1,0:T(8,128)} %get-tuple-element.12) | copy-start | bytes 6291460
  197.2 1.3 copy-start.3
Sparse Core Ops, SparseCore 0:
  9.6 106.1 all-gather.1
